TPU v7x, 32 devices: a whole 2x2x4 slice. The times are simulated.
32 devices in a mesh: group: 2 (over y), gx: 16 (over z, x, core).
Axes of the slice: x: 2, y: 2, z: 4, core: 2. Of those that a mesh axis runs over, the one named last changes fastest.
Arguments:
- step_inputs: bfloat16 [2, 8, 8192], P(None, 'group'), parts along dimension 1, may hold values from -6 to 6
- mlp_inputs: bfloat16 [2, 8, 8192], P(None, 'group'), parts along dimension 1, may hold values from -6 to 6
- qkv_held: bfloat16 [10240, 8192], P('gx'), may hold values from -0.0625 to 0.0625
- gu_held: bfloat16 [28672, 8192], P('gx'), may hold values from -0.0625 to 0.0625
- old_owner: int32 [16], replicated, may hold values from 0 to 15, each once
- new_owner: int32 [16], replicated, may hold values from 0 to 15, each once
- kv_cache: bfloat16 [32768, 2048], P(('group', 'gx')), parts along dimension 0, may hold values from -500 to 500, as said below
- lengths: int32 [8], P('group'), parts along dimension 0, may hold values from 1 to 4096, as said below
Outputs:
- context: bfloat16 [2, 8, 8192], P(None, 'group'), parts along dimension 1
- activation: bfloat16 [2, 8, 14336], P(None, 'group'), parts along dimension 1
- qkv_tiles: bfloat16 [16384, 10240], P(('group', 'gx')), parts along dimension 0
- gu_tiles: bfloat16 [16384, 28672], P(('group', 'gx')), parts along dimension 0
There are 2 independent parts, one for each index of `group`. A program takes and returns all parts, laid end to end along the dimension named above; an argument that names none is the same for every part. Nothing has to cross between parts.
Inputs may be any that keep to these rules, and one draw needn't show every extreme that they name: Request b's cached tokens are kv_cache rows b * 4096 + t for t < lengths[b]; some request holds all 4096. `kv_cache`: each row holds 8 key heads then 8 value heads of 128 entries.
All inputs are finite; a program needn't handle non-finite values.
Results may differ from a plain program's by a relative error of at most 0.03.
Values may be sent and summed in bfloat16 or wider, within the bound.
A program may use at most 320 MiB of HBM per device.

v0:
```python
import jax
import jax.numpy as jnp
from jax import lax
from jax.sharding import PartitionSpec as P

H = 64
KVH = 8
HD = 128
CTX = 4096
ROWS = 4


very_negative = -1e30


def merged(value, axis, join):
    gathered = jax.tree.map(
        lambda a, kind: lax.all_gather(a.astype(kind), axis),
        value,
        (jnp.bfloat16, jnp.bfloat16, jnp.bfloat16),
    )

    def take(source):
        return jax.tree.map(
            lambda a, own: lax.dynamic_index_in_dim(a, source, 0, False).astype(own.dtype),
            gathered,
            value,
        )

    return lax.fori_loop(
        1, lax.axis_size(axis), lambda source, state: join(state, take(source)), take(0)
    )


def reorder_pieces(held, order, devices):
    height = held.shape[0]
    return held.reshape(height, devices, -1)[:, order, :].reshape(height, -1)


def settle_blocks(received, order, devices):
    height, breadth = received.shape
    placed = received.reshape(devices, height // devices, breadth)[order]
    return placed.reshape(height, breadth).T


def join_partials(earlier, later_part):
    top_early, total_early, numer_early = earlier
    top_late, total_late, numer_late = later_part
    joined_top = jnp.maximum(top_early, top_late)
    factor_early = jnp.exp(top_early - joined_top)
    factor_late = jnp.exp(top_late - joined_top)
    joined_total = total_early * factor_early + total_late * factor_late
    joined_numer = numer_early * factor_early[..., None] + numer_late * factor_late[..., None]
    return (joined_top, joined_total, joined_numer)


def local(step_inputs, mlp_inputs, qkv_held, gu_held, old_owner, new_owner, kv_cache, lengths):
    devices = lax.axis_size("gx")
    myself = lax.axis_index("gx")
    model_width = step_inputs.shape[2]
    in_block = model_width // devices
    new_inverse = jnp.argsort(new_owner)
    qkv_send = reorder_pieces(qkv_held, new_inverse, devices)
    gu_send = reorder_pieces(gu_held, new_inverse, devices)
    qkv_recv, gu_recv = (
        lax.all_to_all(qkv_send, "gx", split_axis=1, concat_axis=0, tiled=True),
        lax.all_to_all(gu_send, "gx", split_axis=1, concat_axis=0, tiled=True),
    )
    qkv_tiles = settle_blocks(qkv_recv, old_owner, devices)
    gu_tiles = settle_blocks(gu_recv, old_owner, devices)
    my_block = jnp.sum(jnp.where(new_owner == myself, jnp.arange(devices, dtype=jnp.int32), 0))
    start = my_block * in_block
    step_slice = lax.dynamic_slice_in_dim(step_inputs, start, in_block, 2)
    mlp_slice = lax.dynamic_slice_in_dim(mlp_inputs, start, in_block, 2)
    qkv_term = jnp.einsum("srd,dc->src", step_slice, qkv_tiles, preferred_element_type=jnp.float32)
    gu_term = jnp.einsum("srd,dc->src", mlp_slice, gu_tiles, preferred_element_type=jnp.float32)
    qkv_total, gu_total = lax.psum((qkv_term, gu_term), "gx")
    projected = qkv_total.astype(jnp.bfloat16)
    activation = (jax.nn.silu(gu_total[..., 0::2]) * gu_total[..., 1::2]).astype(jnp.bfloat16)
    score_scale = 1.0 / HD**0.5
    group_size = H // KVH
    local_tokens = kv_cache.shape[0]
    first_token = myself * local_tokens
    row_index = first_token // CTX
    offset = first_token % CTX
    queries = projected[..., : H * HD].reshape(2, ROWS, KVH, group_size, HD)
    new_keys = projected[..., H * HD : (H + KVH) * HD].reshape(2, ROWS, KVH, HD)
    new_values = projected[..., (H + KVH) * HD :].reshape(2, ROWS, KVH, HD)
    row_query = lax.dynamic_index_in_dim(queries, row_index, 1, keepdims=False)
    cache_keys = kv_cache[:, : KVH * HD].reshape(local_tokens, KVH, HD)
    cache_values = kv_cache[:, KVH * HD :].reshape(local_tokens, KVH, HD)
    scores = (
        jnp.einsum("sgqd,tgd->sgqt", row_query, cache_keys, preferred_element_type=jnp.float32)
        * score_scale
    )
    row_length = lax.dynamic_index_in_dim(lengths, row_index, 0, keepdims=False)
    valid = offset + jnp.arange(local_tokens, dtype=jnp.int32) < row_length
    scores = jnp.where(valid[None, None, None, :], scores, very_negative)
    local_top = jnp.max(scores, axis=3)
    weights = jnp.where(valid[None, None, None, :], jnp.exp(scores - local_top[..., None]), 0.0)
    local_total = jnp.sum(weights, axis=3)
    local_numer = jnp.einsum(
        "sgqt,tgd->sgqd",
        weights.astype(jnp.bfloat16),
        cache_values,
        preferred_element_type=jnp.float32,
    )
    owner_rows = jnp.arange(ROWS, dtype=jnp.int32) == row_index
    top_full = jnp.where(owner_rows[None, :, None, None], local_top[:, None], very_negative)
    total_full = jnp.where(owner_rows[None, :, None, None], local_total[:, None], 0.0)
    numer_full = jnp.where(owner_rows[None, :, None, None, None], local_numer[:, None], 0.0)
    top_all, total_all, numer_all = merged((top_full, total_full, numer_full), "gx", join_partials)
    new_scores = (
        jnp.einsum("srgqd,jrgd->srgqj", queries, new_keys, preferred_element_type=jnp.float32)
        * score_scale
    )
    causal = jnp.arange(2)[None, :] <= jnp.arange(2)[:, None]
    causal_mask = causal[:, None, None, None, :]
    new_scores = jnp.where(causal_mask, new_scores, very_negative)
    overall = jnp.maximum(top_all, jnp.max(new_scores, axis=4))
    new_weights = jnp.where(causal_mask, jnp.exp(new_scores - overall[..., None]), 0.0)
    carried = jnp.exp(top_all - overall)
    total = total_all * carried + jnp.sum(new_weights, axis=4)
    numer = numer_all * carried[..., None]
    numer = numer + jnp.einsum(
        "srgqj,jrgd->srgqd",
        new_weights.astype(jnp.bfloat16),
        new_values,
        preferred_element_type=jnp.float32,
    )
    context = (numer / total[..., None]).astype(jnp.bfloat16).reshape(2, ROWS, H * HD)
    return (context, activation, qkv_tiles, gu_tiles)


def solution(mesh):
    return jax.shard_map(
        local,
        mesh=mesh,
        in_specs=(
            P(None, "group", None),
            P(None, "group", None),
            P("gx", None),
            P("gx", None),
            P(),
            P(),
            P(("group", "gx"), None),
            P("group"),
        ),
        out_specs=(
            P(None, "group", None),
            P(None, "group", None),
            P(("group", "gx"), None),
            P(("group", "gx"), None),
        ),
        check_vma=False,
    )
```

profile of v0, /device:TPU:8, one launch (start us, length us, event | category | flops | bytes accessed | tf_op | source)
XLA Modules:
  0.0 1242.5 jit_solution(14873286824371901983)
XLA Ops:
  7.2 1.9 sort.17
  9.1 1.3 compare_select_fusion.1
  10.4 14.6 %copy.85 = bf16[640,8192]{0,1:T(8,128)(2,1)} copy(bf16[640,8192]{1,0:T(8,128)(2,1)} %param.12) | data formatting | bytes 20971520 | tf_op args[2]
  25.0 15.1 %copy.86 = bf16[640,16,512]{2,0,1:T(8,128)(2,1)} copy(bf16[640,16,512]{0,2,1:T(8,128)(2,1)} %bitcast.93) | data formatting | bytes 20971520 | tf_op jit(solution)/shard_map/reshape | solution.py:37
  40.1 9.8 gather_fusion
  50.0 6.3 all-to-all-start
  56.2 35.9 %copy.105 = bf16[1792,8192]{0,1:T(8,128)(2,1)} copy(bf16[1792,8192]{1,0:T(8,128)(2,1)} %param.13) | data formatting | bytes 58720256 | tf_op args[3]
  92.1 20.9 %gather_fusion.2 = bf16[16,1792,512]{1,2,0:T(8,128)(2,1)} fusion(bf16[1792,16,512]{0,2,1:T(8,128)(2,1)} %bitcast.89, s32[1024]{0:T(1024)S(1)} %pad_clamp_fusion.1), kind=kCustom, calls=%fused_computation.2 | custom fusion | bytes 58720320 | tf_op jit(solution)/shard_map/gather | solution.py:37
  112.9 168.9 %all-to-all-done = bf16[640,16,512]{2,0,1:T(8,128)(2,1)} async-done(((bf16[640,16,512]{2,0,1:T(8,128)(2,1)}), bf16[640,16,512]{2,0,1:T(8,128)(2,1)}, u32[]{:S(2)}, u32[]{:S(2)}) %all-to-all-start) | async-done | bytes 10485792 | tf_op jit(solution)/shard_map/all_to_all | solution.py:66
  281.9 6.6 all-to-all-start.1
  289.2 4.7 fusion.38
  293.8 2.9 copy.122
  296.7 3.9 copy.121
  301.9 9.8 gather_fusion.1
  311.7 6.9 fusion.29
  318.6 640.2 %all-reduce.4 = bf16[2,4,10240]{2,1,0:T(4,128)(2,1)S(1)} all-reduce(f32[2,4,10240]{2,1,0:T(4,128)S(1)} %fusion.29), channel_id=1, replica_groups=mesh['group'=2,'gx'=16] {'gx'}, use_global_device_ids=true, to_apply=%region_2.3 | all-reduce | flops 81920 | bytes 491520 | tf_op jit(solution)/shard_map/psum | solution.py:77
  959.0 2.1 fusion.40
  962.9 13.7 %copy.107 = bf16[10240,512]{0,1:T(8,128)(2,1)} copy(bf16[10240,512]{1,0:T(8,128)(2,1)} %bitcast.91) | data formatting | bytes 20971520 | tf_op jit(solution)/shard_map/reshape | solution.py:43
  976.8 18.9 %all_gather.13 = bf16[16,2,4,8,8]{4,3,2,1,0:T(8,128)(2,1)S(1)} all-gather(bf16[1,2,4,8,8]{4,3,2,1,0:T(8,128)(2,1)S(1)} %get-tuple-element.223), channel_id=1, replica_groups=mesh['group'=2,'gx'=16] {'gx'}, dimensions={0}, use_global_device_ids=true | all-gather | bytes 17408 | tf_op jit(solution)/shard_map/all_gather | solution.py:18
  995.6 19.7 %all_gather.12 = bf16[16,2,4,8,8]{4,3,2,1,0:T(8,128)(2,1)S(1)} all-gather(bf16[1,2,4,8,8]{4,3,2,1,0:T(8,128)(2,1)S(1)} %get-tuple-element.224), channel_id=1, replica_groups=mesh['group'=2,'gx'=16] {'gx'}, dimensions={0}, use_global_device_ids=true | all-gather | bytes 17408 | tf_op jit(solution)/shard_map/all_gather | solution.py:18
  1017.0 18.7 %while.19 = (s32[]{:T(128)}, f32[2,4,8,8]{3,2,1,0:T(8,128)S(1)}, f32[2,4,8,8]{3,2,1,0:T(8,128)S(1)}, f32[2,4,8,8,128]{4,3,2,1,0:T(8,128)S(1)}, bf16[16,2,4,8,8]{...) while((s32[]{:T(128)}, f32[2,4,8,8]{3,2,1,0:T(8,128)S(1)}, ...), condition=%wide.region_6.7_spmd, body=%wide.region_5.6_spmd.sunk | while | flops 266245 | bytes 673935 | solution.py:30
  1017.0 1.2 fusion.50
  1018.3 1.2 fusion.50
  1020.8 1.2 fusion.50
  1022.0 1.2 fusion.50
  1035.9 21.3 %gather_fusion.3 = bf16[16,1792,512]{1,2,0:T(8,128)(2,1)} fusion(bf16[16,1792,512]{1,2,0:T(8,128)(2,1)} %bitcast.26, s32[1024]{0:T(1024)S(1)} %pad_clamp_fusion), kind=kCustom, calls=%fused_computation.3 | custom fusion | bytes 58720320 | tf_op jit(solution)/shard_map/gather | solution.py:42
  1057.2 36.0 %copy.106 = bf16[16,1792,512]{2,1,0:T(8,128)(2,1)} copy(bf16[16,1792,512]{1,2,0:T(8,128)(2,1)} %gather_fusion.3) | data formatting | bytes 58720256 | tf_op jit(solution)/shard_map/gather | solution.py:42
  1093.2 14.6 %fusion.27 = f32[2,4,28672]{2,1,0:T(4,128)} fusion(bf16[28672,512,1]{1,0,2:T(8,128)(2,1)} %bitcast.86, bf16[2,4,8192]{2,1,0:T(4,128)(2,1)S(1)} %copy-done, s32[]{:T(128)S(6)} %select_n.103), kind=kOutput, calls=%fused_computation.52 | convolution fusion | flops 234881024 | bytes 30285828 | tf_op jit(solution)/shard_map/srd,dc->src/dot_general | solution.py:76
  1109.0 36.3 %copy.108 = bf16[512,28672]{1,0:T(8,128)(2,1)} copy(bf16[512,28672]{0,1:T(8,128)(2,1)} %bitcast.87) | data formatting | bytes 58720256
  1145.3 55.9 %all-reduce.3.cloned.1.call-done = f32[2,4,28672]{2,1,0:T(4,128)} async-done(((f32[2,4,28672]{2,1,0:T(4,128)}), f32[2,4,28672]{2,1,0:T(4,128)}) %all-reduce.3.cloned.1.call-update) | async-done | bytes 917520 | tf_op jit(solution)/shard_map/psum | solution.py:77
  1201.1 16.8 %slice.30 = f32[2,4,14336]{2,1,0:T(4,128)S(1)} slice(f32[2,4,28672]{2,1,0:T(4,128)} %all-reduce.3.cloned.1.call-done), slice={[0:2:1], [0:4:1], [1:28672:2]} | slice | bytes 917504 | tf_op jit(solution)/shard_map/slice | solution.py:79
  1217.9 16.8 %slice.29 = f32[2,4,14336]{2,1,0:T(4,128)S(1)} slice(f32[2,4,28672]{2,1,0:T(4,128)} %all-reduce.3.cloned.1.call-done), slice={[0:2:1], [0:4:1], [0:28672:2]} | slice | bytes 917504 | tf_op jit(solution)/shard_map/slice | solution.py:79
  (71 shorter events, 20.9 us)
Async XLA Ops:
  7.2 1086.1 %copy-start = (bf16[2,4,8192]{2,1,0:T(4,128)(2,1)S(1)}, bf16[2,4,8192]{2,1,0:T(4,128)(2,1)}, u32[]{:S(2)}) copy-start(bf16[2,4,8192]{2,1,0:T(4,128)(2,1)} %param.11) | copy-start | bytes 393220
  50.0 231.9 %all-to-all-start = ((bf16[640,16,512]{2,0,1:T(8,128)(2,1)}), bf16[640,16,512]{2,0,1:T(8,128)(2,1)}, u32[]{:S(2)}, u32[]{:S(2)}) async-start(bf16[640,16,512]{2,0,1:T(8,128)(2,1)} %bitcast.92), calls=%async_computation | async-start | bytes 20971520 | tf_op jit(solution)/shard_map/all_to_all | solution.py:66
  281.9 754.0 %all-to-all-start.1 = ((bf16[1792,16,512]{0,2,1:T(8,128)(2,1)}), bf16[1792,16,512]{0,2,1:T(8,128)(2,1)}, u32[]{:S(2)}, u32[]{:S(2)}) async-start(bf16[1792,16,512]{0,2,1:T(8,128)(2,1)} %bitcast.88), calls=%async_computation.1 | async-start | bytes 58720256 | tf_op jit(solution)/shard_map/all_to_all | solution.py:67
  288.4 12.2 copy-start.1
  288.4 13.5 %copy-start.2 = (s32[16]{0:T(128)S(1)}, s32[16]{0:T(128)}, u32[]{:S(2)}) copy-start(s32[16]{0:T(128)} %param.14) | copy-start | bytes 196
  288.4 727.6 %all-gather.2.cloned.1.call-start = ((), (), s32[]{:S(2)}) async-start(), calls=%async_computation.2 | async-start | bytes 2228224 | tf_op jit(solution)/shard_map/all_gather | solution.py:18
  962.6 238.6 %all-reduce.3.cloned.1.call-start = ((), (), s32[]{:S(2)}) async-start(), calls=%async_computation.3 | async-start | bytes 1835008 | tf_op jit(solution)/shard_map/psum | solution.py:77
Sparse Core Ops, SparseCore 0:
  962.7 43.5 all-gather.1
  1107.9 93.1 all-reduce.2
where the time goes:
time: 1250 us; the launch traced here: 1240 us
  blocking collectives  679 us (54%)
  local copies, waits for them, and re-layouts  260 us (21%)
  waiting for transfers between devices  225 us (18%)
  other arithmetic  25.2 us (2%)
  matrix products  25.2 us (2%)
  between operations  15 us (1%)
  starting transfers between devices  12.9 us (1%)
    psum x1, blocking collectives, local(): qkv_total, gu_total = lax.psum((qkv_term, gu_term), 'gx')  640 us
    all_to_all x1, waiting for transfers between devices, local(): lax.all_to_all(qkv_send, 'gx', split_axis=1, concat_axis=0, tiled=True)  169 us
    unnamed x11, local copies, waits for them, and re-layouts  93.6 us
    gather x3, local copies, waits for them, and re-layouts, settle_blocks(): placed = received.reshape(devices, height // devices, breadth)[order]  67.1 us
    psum x1, waiting for transfers between devices, local(): qkv_total, gu_total = lax.psum((qkv_term, gu_term), 'gx')  55.9 us
    all_gather x2, blocking collectives, merged(): lax.all_gather(a.astype(kind), axis)  38.5 us
    gather x2, local copies, waits for them, and re-layouts, reorder_pieces(): return held.reshape(height, devices, -1)[:, order, :].reshape(height, -1)  30.7 us
  transfers between devices with their start and end apart: 4, of which 2 were waited for; matrix products, arithmetic and copies ran while one was open for 13% of the time, Pallas kernels for 0%

commit v1 on v0

v1 whole, which is shorter than its diff:
```python
import functools

import jax
import jax.numpy as jnp
from jax import lax
from jax.experimental import pallas as pl
from jax.experimental.pallas import tpu as pltpu
from jax.sharding import PartitionSpec as P

H = 64
KVH = 8
HD = 128
CTX = 4096
ROWS = 4

very_negative = -1e30


def reorder_pieces(held, order, devices):
    height = held.shape[0]
    return held.reshape(height, devices, -1)[:, order, :].reshape(height, -1)


def settle_blocks(received, order, devices):
    height, breadth = received.shape
    placed = received.reshape(devices, height // devices, breadth)[order]
    return placed.reshape(height, breadth).T


def plain_tiles(held, new_inverse, old_owner, devices):
    sent = reorder_pieces(held, new_inverse, devices)
    received = lax.all_to_all(sent, "gx", split_axis=1, concat_axis=0, tiled=True)
    return settle_blocks(received, old_owner, devices)


def turn_kernel(columns, held_ref, out_ref):
    out_ref[0] = held_ref[...].T


def turn_pieces(held, columns, first, count, half):
    devices = columns.shape[0]
    return pl.pallas_call(
        turn_kernel,
        grid_spec=pltpu.PrefetchScalarGridSpec(
            num_scalar_prefetch=1,
            grid=(devices,),
            in_specs=[pl.BlockSpec((count, half), lambda p, columns: (first // count, columns[p]))],
            out_specs=pl.BlockSpec((1, half, count), lambda p, columns: (p, 0, 0)),
        ),
        out_shape=jax.ShapeDtypeStruct((devices, half, count), held.dtype),
        cost_estimate=pl.CostEstimate(
            flops=0, bytes_accessed=4 * devices * half * count, transcendentals=0
        ),
    )(columns, held)


def place_kernel(devices, half, height, first, count, order, which, *refs):
    source, tile, sems = refs[0], refs[-2], refs[-1]
    row = pl.multiple_of(which[0] * half, half)
    copies = []
    for c in range(devices):
        copy = pltpu.make_async_copy(
            source.at[order[c]],
            tile.at[pl.ds(row, half), pl.ds(c * height + first, count)],
            sems.at[c],
        )
        copy.start()
        copies.append(copy)
    for copy in copies:
        copy.wait()


def place_blocks(source, tile, order, which, height, first):
    devices, half, count = source.shape
    smem = pl.BlockSpec(memory_space=pltpu.SMEM)
    anywhere = pl.BlockSpec(memory_space=pl.ANY)
    operands = [order, which.reshape(1), source]
    aliases = {}
    if tile is not None:
        operands.append(tile)
        aliases = {3: 0}
    return pl.pallas_call(
        functools.partial(place_kernel, devices, half, height, first, count),
        out_shape=jax.ShapeDtypeStruct((2 * half, devices * height), source.dtype),
        in_specs=[smem, smem] + [anywhere] * (len(operands) - 2),
        out_specs=anywhere,
        scratch_shapes=[pltpu.SemaphoreType.DMA((devices,))],
        input_output_aliases=aliases,
        cost_estimate=pl.CostEstimate(
            flops=0, bytes_accessed=4 * devices * half * count, transcendentals=0
        ),
    )(*operands)


def shared_tiles(qkv_held, gu_held, new_inverse, old_owner, devices):
    mine = lax.axis_index("group")
    half = qkv_held.shape[1] // devices // 2
    columns = 2 * new_inverse.astype(jnp.int32) + mine
    chunks = [(1, 0, 512), (1, 512, 512), (1, 1024, 512), (0, 0, 512), (1, 1536, 256), (0, 512, 128)]
    held = (qkv_held, gu_held)
    tiles = [None, None]
    for which, first, count in chunks:
        sent = turn_pieces(held[which], columns, first, count, half)
        own = lax.all_to_all(sent, "gx", split_axis=0, concat_axis=0, tiled=True)
        other = lax.ppermute(own, "group", [(0, 1), (1, 0)])
        height = held[which].shape[0]
        tiles[which] = place_blocks(own, tiles[which], old_owner, mine, height, first)
        tiles[which] = place_blocks(other, tiles[which], old_owner, 1 - mine, height, first)
    return tiles


def gathered_columns(part, old_owner):
    steps, rows, width = part.shape
    blocks = lax.all_gather(part, "gx")[old_owner]
    return jnp.moveaxis(blocks, 0, 2).reshape(steps, rows, -1)


def local(step_inputs, mlp_inputs, qkv_held, gu_held, old_owner, new_owner, kv_cache, lengths):
    devices = lax.axis_size("gx")
    groups = lax.axis_size("group")
    myself = lax.axis_index("gx")
    in_block = qkv_held.shape[1] // devices
    new_inverse = jnp.argsort(new_owner)
    if groups == 2 and in_block == 512 and qkv_held.shape[0] == 640 and gu_held.shape[0] == 1792:
        qkv_tiles, gu_tiles = shared_tiles(qkv_held, gu_held, new_inverse, old_owner, devices)
    else:
        qkv_tiles = plain_tiles(qkv_held, new_inverse, old_owner, devices)
        gu_tiles = plain_tiles(gu_held, new_inverse, old_owner, devices)
    qkv_part = jnp.einsum("srd,cd->src", step_inputs, qkv_held, preferred_element_type=jnp.float32)
    projected = gathered_columns(qkv_part.astype(jnp.bfloat16), old_owner)
    gu_part = jnp.einsum("srd,cd->src", mlp_inputs, gu_held, preferred_element_type=jnp.float32)
    activated = (jax.nn.silu(gu_part[..., 0::2]) * gu_part[..., 1::2]).astype(jnp.bfloat16)
    activation = gathered_columns(activated, old_owner)
    score_scale = 1.0 / HD**0.5
    group_size = H // KVH
    local_tokens = kv_cache.shape[0]
    first_token = myself * local_tokens
    row_index = first_token // CTX
    offset = first_token % CTX
    queries = projected[..., : H * HD].reshape(2, ROWS, KVH, group_size, HD)
    new_keys = projected[..., H * HD : (H + KVH) * HD].reshape(2, ROWS, KVH, HD)
    new_values = projected[..., (H + KVH) * HD :].reshape(2, ROWS, KVH, HD)
    row_query = lax.dynamic_index_in_dim(queries, row_index, 1, keepdims=False)
    cache_keys = kv_cache[:, : KVH * HD].reshape(local_tokens, KVH, HD)
    cache_values = kv_cache[:, KVH * HD :].reshape(local_tokens, KVH, HD)
    scores = (
        jnp.einsum("sgqd,tgd->sgqt", row_query, cache_keys, preferred_element_type=jnp.float32)
        * score_scale
    )
    row_length = lax.dynamic_index_in_dim(lengths, row_index, 0, keepdims=False)
    valid = offset + jnp.arange(local_tokens, dtype=jnp.int32) < row_length
    scores = jnp.where(valid[None, None, None, :], scores, very_negative)
    local_top = jnp.max(scores, axis=3)
    weights = jnp.where(valid[None, None, None, :], jnp.exp(scores - local_top[..., None]), 0.0)
    local_total = jnp.sum(weights, axis=3)
    local_numer = jnp.einsum(
        "sgqt,tgd->sgqd",
        weights.astype(jnp.bfloat16),
        cache_values,
        preferred_element_type=jnp.float32,
    )
    shards = CTX // local_tokens
    pair_all = lax.all_gather(jnp.stack([local_top, local_total]), "gx")
    pair_all = pair_all.reshape(ROWS, shards, 2, 2, KVH, group_size)
    numer_parts = lax.all_gather(local_numer.astype(jnp.bfloat16), "gx")
    numer_parts = numer_parts.reshape(ROWS, shards, 2, KVH, group_size, HD)
    tops, totals = pair_all[:, :, 0], pair_all[:, :, 1]
    top_all = jnp.max(tops, axis=1)
    factors = jnp.exp(tops - top_all[:, None])
    total_all = jnp.moveaxis(jnp.sum(totals * factors, axis=1), 0, 1)
    numer_all = jnp.sum(numer_parts.astype(jnp.float32) * factors[..., None], axis=1)
    numer_all = jnp.moveaxis(numer_all, 0, 1)
    top_all = jnp.moveaxis(top_all, 0, 1)
    new_scores = (
        jnp.einsum("srgqd,jrgd->srgqj", queries, new_keys, preferred_element_type=jnp.float32)
        * score_scale
    )
    causal = jnp.arange(2)[None, :] <= jnp.arange(2)[:, None]
    causal_mask = causal[:, None, None, None, :]
    new_scores = jnp.where(causal_mask, new_scores, very_negative)
    overall = jnp.maximum(top_all, jnp.max(new_scores, axis=4))
    new_weights = jnp.where(causal_mask, jnp.exp(new_scores - overall[..., None]), 0.0)
    carried = jnp.exp(top_all - overall)
    total = total_all * carried + jnp.sum(new_weights, axis=4)
    numer = numer_all * carried[..., None]
    numer = numer + jnp.einsum(
        "srgqj,jrgd->srgqd",
        new_weights.astype(jnp.bfloat16),
        new_values,
        preferred_element_type=jnp.float32,
    )
    context = (numer / total[..., None]).astype(jnp.bfloat16).reshape(2, ROWS, H * HD)
    return (context, activation, qkv_tiles, gu_tiles)


def solution(mesh):
    return jax.shard_map(
        local,
        mesh=mesh,
        in_specs=(
            P(None, "group", None),
            P(None, "group", None),
            P("gx", None),
            P("gx", None),
            P(),
            P(),
            P(("group", "gx"), None),
            P("group"),
        ),
        out_specs=(
            P(None, "group", None),
            P(None, "group", None),
            P(("group", "gx"), None),
            P(("group", "gx"), None),
        ),
        check_vma=False,
    )
```

time: 1250 us -> 1840 us (1.47)
  Pallas kernels: 0 us -> 1300 us
  blocking collectives: 679 us -> 113 us
  local copies, waits for them, and re-layouts: 260 us -> 18.6 us
  waiting for transfers between devices: 225 us -> 331 us
  starting transfers between devices: 12.9 us -> 44 us
  other arithmetic: 25.2 us -> 3.97 us
    pallas_call x0 -> x18, Pallas kernels: none -> 1300 us  [the longest x12 1230 us: place_blocks(): pl.pallas_call(functools.partial(place_kernel, devices, half, height, fir...]
    psum x1 -> x0, blocking collectives: 640 us -> none  [local(): qkv_total, gu_total = lax.psum((qkv_term, gu_term), 'gx')]
    all_to_all x2 -> x6, waiting for transfers between devices: 169 us -> 318 us  [shared_tiles(): own = lax.all_to_all(sent, 'gx', split_axis=0, concat_axis=0, tiled=True)]
    gather x5 -> x2, local copies, waits for them, and re-layouts: 97.8 us -> 1.45 us  [gathered_columns(): blocks = lax.all_gather(part, 'gx')[old_owner]]
    unnamed x11 -> x14, local copies, waits for them, and re-layouts: 93.6 us -> 7.94 us
    all_gather x2 -> x4, blocking collectives: 38.5 us -> 113 us  [the longest x2 59.3 us: gathered_columns(): blocks = lax.all_gather(part, 'gx')[old_owner]]
    psum x1 -> x0, waiting for transfers between devices: 55.9 us -> none  [local(): qkv_total, gu_total = lax.psum((qkv_term, gu_term), 'gx')]
    slice x3, local copies, waits for them, and re-layouts: 38.2 us -> 6.73 us  [the longest x1 4.67 us: local(): cache_keys = kv_cache[:, :KVH * HD].reshape(local_tokens, KVH, HD)]
  transfers between devices with their start and end apart: 4 -> 12, of which waited for: 2 -> 5; matrix products, arithmetic and copies ran while one was open for 13% -> 2% of each run, Pallas kernels for 0% -> 68%
where the time goes in v1:
time: 1840 us; the launch traced here: 1830 us
  Pallas kernels  1300 us (71%)
  waiting for transfers between devices  331 us (18%)
  blocking collectives  113 us (6%)
  starting transfers between devices  44 us (2%)
  matrix products  25.7 us (1%)
  local copies, waits for them, and re-layouts  18.6 us (1%)
    pallas_call x12, Pallas kernels, place_blocks(): pl.pallas_call(functools.partial(place_kernel, devices, half, height, fir...  1230 us
    all_to_all x6, waiting for transfers between devices, shared_tiles(): own = lax.all_to_all(sent, 'gx', split_axis=0, concat_axis=0, tiled=True)  318 us
    pallas_call x6, Pallas kernels, turn_pieces(): pl.pallas_call(turn_kernel, grid_spec=pltpu.PrefetchScalarGridSpec(num_sc...  66.7 us
    all_gather x2, blocking collectives, gathered_columns(): blocks = lax.all_gather(part, 'gx')[old_owner]  59.3 us
  transfers between devices with their start and end apart: 12, of which 5 were waited for; matrix products, arithmetic and copies ran while one was open for 2% of the time, Pallas kernels for 68%

profile of v1, /device:TPU:8, one launch (start us, length us, event | category | flops | bytes accessed | tf_op | source)
XLA Modules:
  0.0 1834.4 jit_solution(8844595878249875654)
XLA Ops:
  3.1 11.5 shard_map.120
  20.9 11.5 shard_map.119
  32.4 79.3 %all-to-all-done.5.refs_0_ = bf16[16,256,512]{2,1,0:T(8,128)(2,1)} async-done(((bf16[16,256,512]{2,1,0:T(8,128)(2,1)}), bf16[16,256,512]{2,1,0:T(8,128)(2,1)}, u32[]{:S(2)}, u32[]{:S(2)}) %all-to-all-start.5) | async-done | bytes 4194336 | tf_op jit(solution)/shard_map/all_to_all | solution.py:104
  111.7 6.6 all-to-all-start.4
  118.3 11.5 shard_map.118
  129.8 79.3 %all-to-all-done.4.refs_0_ = bf16[16,256,512]{2,1,0:T(8,128)(2,1)} async-done(((bf16[16,256,512]{2,1,0:T(8,128)(2,1)}), bf16[16,256,512]{2,1,0:T(8,128)(2,1)}, u32[]{:S(2)}, u32[]{:S(2)}) %all-to-all-start.4) | async-done | bytes 4194336 | tf_op jit(solution)/shard_map/all_to_all | solution.py:104
  209.1 6.6 all-to-all-start.3
  215.6 11.5 shard_map.112
  227.1 79.3 %all-to-all-done.3.refs_0_ = bf16[16,256,512]{2,1,0:T(8,128)(2,1)} async-done(((bf16[16,256,512]{2,1,0:T(8,128)(2,1)}), bf16[16,256,512]{2,1,0:T(8,128)(2,1)}, u32[]{:S(2)}, u32[]{:S(2)}) %all-to-all-start.3) | async-done | bytes 4194336 | tf_op jit(solution)/shard_map/all_to_all | solution.py:104
  306.5 6.6 all-to-all-start.1
  313.0 10.6 shard_map.117
  323.6 80.2 %all-to-all-done.1.refs_0_ = bf16[16,256,512]{2,1,0:T(8,128)(2,1)} async-done(((bf16[16,256,512]{2,1,0:T(8,128)(2,1)}), bf16[16,256,512]{2,1,0:T(8,128)(2,1)}, u32[]{:S(2)}, u32[]{:S(2)}) %all-to-all-start.1) | async-done | bytes 4194336 | tf_op jit(solution)/shard_map/all_to_all | solution.py:104
  410.4 10.0 shard_map.111
  420.4 6.9 fusion.12
  427.3 41.2 %all-gather = bf16[32,4,640]{2,1,0:T(4,128)(2,1)S(1)} all-gather(bf16[2,4,640]{2,1,0:T(4,128)(2,1)S(1)} %fusion.12), channel_id=2, replica_groups=mesh['group'=2,'gx'=16] {'gx'}, dimensions={0}, use_global_device_ids=true | all-gather | bytes 174080 | tf_op jit(solution)/shard_map/all_gather | solution.py:114
  471.1 13.4 fusion
  503.6 35.6 %all-gather.2 = f32[32,2,8,8]{3,2,1,0:T(8,128)S(1)} all-gather(f32[2,2,8,8]{3,2,1,0:T(8,128)S(1)} %pad_maximum_fusion), channel_id=4, replica_groups=mesh['group'=2,'gx'=16] {'gx'}, dimensions={0}, use_global_device_ids=true | all-gather | bytes 17408 | tf_op jit(solution)/shard_map/all_gather | solution.py:163
  550.3 13.0 collective-permute-done.5.refs_0_
  564.8 18.1 all-gather.1
  584.4 18.1 all-gather.3
  604.0 129.0 %shard_map.121.refs_1_ = bf16[512,28672]{1,0:T(8,128)(2,1)} custom-call(s32[16]{0:T(128)} %order.23, s32[1]{0:T(128)} %bitcast.28.which, bf16[16,256,512]{2,1,0:T(8,128)(2,1)} %all-to-all-done.5.refs_0_), custom_call_target="tpu_custom_call" | custom-call | bytes 8388608 | tf_op jit(solution)/shard_map/pallas_call | solution.py:82
  733.0 129.0 %shard_map.113.refs_1_ = bf16[512,10240]{1,0:T(8,128)(2,1)} custom-call(s32[16]{0:T(128)} %order.23, s32[1]{0:T(128)} %bitcast.28.which, bf16[16,256,512]{2,1,0:T(8,128)(2,1)} %all-to-all-done.1.refs_0_), custom_call_target="tpu_custom_call" | custom-call | bytes 8388608 | tf_op jit(solution)/shard_map/pallas_call | solution.py:82
  861.9 129.0 %shard_map.122.refs_1_ = bf16[512,28672]{1,0:T(8,128)(2,1)} custom-call(s32[16]{0:T(128)} %order.23, s32[1]{0:T(128)} %bitcast.27.which, bf16[16,256,512]{2,1,0:T(8,128)(2,1)} %collective-permute-done.5.refs_0_, bf16[512,28672]{1,0:T(8,128)(2,1)} %shard_map.121.refs_1_), custom_call_target="tpu_custom_call", output_to_operand_aliasing={{}: (3, {})} | custom-call | bytes 8388608 | tf_op jit(solution)/shard_map/pallas_call | solution.py:82
  990.9 129.0 %shard_map.123.refs_1_ = bf16[512,28672]{1,0:T(8,128)(2,1)} custom-call(s32[16]{0:T(128)} %order.23, s32[1]{0:T(128)} %bitcast.28.which, bf16[16,256,512]{2,1,0:T(8,128)(2,1)} %all-to-all-done.4.refs_0_, bf16[512,28672]{1,0:T(8,128)(2,1)} %shard_map.122.refs_1_), custom_call_target="tpu_custom_call", output_to_operand_aliasing={{}: (3, {})} | custom-call | bytes 8388608 | tf_op jit(solution)/shard_map/pallas_call | solution.py:82
  1119.9 129.0 %shard_map.124.refs_1_ = bf16[512,28672]{1,0:T(8,128)(2,1)} custom-call(s32[16]{0:T(128)} %order.23, s32[1]{0:T(128)} %bitcast.27.which, bf16[16,256,512]{2,1,0:T(8,128)(2,1)} %collective-permute-done.4.refs_0_, bf16[512,28672]{1,0:T(8,128)(2,1)} %shard_map.123.refs_1_), custom_call_target="tpu_custom_call", output_to_operand_aliasing={{}: (3, {})} | custom-call | bytes 8388608 | tf_op jit(solution)/shard_map/pallas_call | solution.py:82
  1248.9 129.0 %shard_map.125.refs_1_ = bf16[512,28672]{1,0:T(8,128)(2,1)} custom-call(s32[16]{0:T(128)} %order.23, s32[1]{0:T(128)} %bitcast.28.which, bf16[16,256,512]{2,1,0:T(8,128)(2,1)} %all-to-all-done.3.refs_0_, bf16[512,28672]{1,0:T(8,128)(2,1)} %shard_map.124.refs_1_), custom_call_target="tpu_custom_call", output_to_operand_aliasing={{}: (3, {})} | custom-call | bytes 8388608 | tf_op jit(solution)/shard_map/pallas_call | solution.py:82
  1377.9 129.0 %shard_map.126.refs_1_ = bf16[512,28672]{1,0:T(8,128)(2,1)} custom-call(s32[16]{0:T(128)} %order.23, s32[1]{0:T(128)} %bitcast.27.which, bf16[16,256,512]{2,1,0:T(8,128)(2,1)} %collective-permute-done.3.refs_0_, bf16[512,28672]{1,0:T(8,128)(2,1)} %shard_map.125.refs_1_), custom_call_target="tpu_custom_call", output_to_operand_aliasing={{}: (3, {})} | custom-call | bytes 8388608 | tf_op jit(solution)/shard_map/pallas_call | solution.py:82
  1506.8 65.4 %shard_map.127.refs_1_ = bf16[512,28672]{1,0:T(8,128)(2,1)} custom-call(s32[16]{0:T(128)} %order.23, s32[1]{0:T(128)} %bitcast.28.which, bf16[16,256,256]{2,1,0:T(8,128)(2,1)} %copy-done.2, bf16[512,28672]{1,0:T(8,128)(2,1)} %shard_map.126.refs_1_), custom_call_target="tpu_custom_call", output_to_operand_aliasing={{}: (3, {})} | custom-call | bytes 4194304 | tf_op jit(solution)/shard_map/pallas_call | solution.py:82
  1572.3 129.0 %shard_map.114.refs_1_ = bf16[512,10240]{1,0:T(8,128)(2,1)} custom-call(s32[16]{0:T(128)} %order.23, s32[1]{0:T(128)} %bitcast.27.which, bf16[16,256,512]{2,1,0:T(8,128)(2,1)} %collective-permute-done.1.refs_0_, bf16[512,10240]{1,0:T(8,128)(2,1)} %shard_map.113.refs_1_), custom_call_target="tpu_custom_call", output_to_operand_aliasing={{}: (3, {})} | custom-call | bytes 8388608 | tf_op jit(solution)/shard_map/pallas_call | solution.py:82
  1701.3 33.7 %shard_map.115.refs_1_ = bf16[512,10240]{1,0:T(8,128)(2,1)} custom-call(s32[16]{0:T(128)} %order.23, s32[1]{0:T(128)} %bitcast.28.which, bf16[16,256,128]{2,1,0:T(8,128)(2,1)} %all-to-all-done.refs_0_, bf16[512,10240]{1,0:T(8,128)(2,1)} %shard_map.114.refs_1_), custom_call_target="tpu_custom_call", output_to_operand_aliasing={{}: (3, {})} | custom-call | bytes 2097152 | tf_op jit(solution)/shard_map/pallas_call | solution.py:82
  1735.0 65.4 %shard_map.128 = bf16[512,28672]{1,0:T(8,128)(2,1)} custom-call(s32[16]{0:T(128)} %order.23, s32[1]{0:T(128)} %bitcast.27.which, bf16[16,256,256]{2,1,0:T(8,128)(2,1)} %collective-permute-done.2.refs_0_, bf16[512,28672]{1,0:T(8,128)(2,1)} %shard_map.127.refs_1_), custom_call_target="tpu_custom_call", output_to_operand_aliasing={{}: (3, {})} | custom-call | bytes 4194304 | tf_op jit(solution)/shard_map/pallas_call | solution.py:82
  1800.4 33.8 %shard_map.116 = bf16[512,10240]{1,0:T(8,128)(2,1)} custom-call(s32[16]{0:T(128)} %order.23, s32[1]{0:T(128)} %bitcast.27.which, bf16[16,256,128]{2,1,0:T(8,128)(2,1)} %collective-permute-done.refs_0_, bf16[512,10240]{1,0:T(8,128)(2,1)} %shard_map.115.refs_1_), custom_call_target="tpu_custom_call", output_to_operand_aliasing={{}: (3, {})} | custom-call | bytes 2097152 | tf_op jit(solution)/shard_map/pallas_call | solution.py:82
  (70 shorter events, 52.4 us)
Async XLA Ops:
  0.6 470.5 %copy-start = (bf16[2,4,8192]{2,1,0:T(4,128)(2,1)S(1)}, bf16[2,4,8192]{2,1,0:T(4,128)(2,1)}, u32[]{:S(2)}) copy-start(bf16[2,4,8192]{2,1,0:T(4,128)(2,1)} %param.9) | copy-start | bytes 393220
  14.6 97.1 %all-to-all-start.5 = ((bf16[16,256,512]{2,1,0:T(8,128)(2,1)}), bf16[16,256,512]{2,1,0:T(8,128)(2,1)}, u32[]{:S(2)}, u32[]{:S(2)}) async-start(bf16[16,256,512]{2,1,0:T(8,128)(2,1)} %shard_map.120), calls=%async_computation.5 | async-start | bytes 8388608 | tf_op jit(solution)/shard_map/all_to_all | solution.py:104
  111.7 97.4 %all-to-all-start.4 = ((bf16[16,256,512]{2,1,0:T(8,128)(2,1)}), bf16[16,256,512]{2,1,0:T(8,128)(2,1)}, u32[]{:S(2)}, u32[]{:S(2)}) async-start(bf16[16,256,512]{2,1,0:T(8,128)(2,1)} %shard_map.119), calls=%async_computation.4 | async-start | bytes 8388608 | tf_op jit(solution)/shard_map/all_to_all | solution.py:104
  209.1 97.4 %all-to-all-start.3 = ((bf16[16,256,512]{2,1,0:T(8,128)(2,1)}), bf16[16,256,512]{2,1,0:T(8,128)(2,1)}, u32[]{:S(2)}, u32[]{:S(2)}) async-start(bf16[16,256,512]{2,1,0:T(8,128)(2,1)} %shard_map.118), calls=%async_computation.3 | async-start | bytes 8388608 | tf_op jit(solution)/shard_map/all_to_all | solution.py:104
  306.5 97.4 %all-to-all-start.1 = ((bf16[16,256,512]{2,1,0:T(8,128)(2,1)}), bf16[16,256,512]{2,1,0:T(8,128)(2,1)}, u32[]{:S(2)}, u32[]{:S(2)}) async-start(bf16[16,256,512]{2,1,0:T(8,128)(2,1)} %shard_map.112), calls=%async_computation.1 | async-start | bytes 8388608 | tf_op jit(solution)/shard_map/all_to_all | solution.py:104
  403.8 95.2 %all-to-all-start.2 = ((bf16[16,256,256]{2,1,0:T(8,128)(2,1)}), bf16[16,256,256]{2,1,0:T(8,128)(2,1)S(1)}, u32[]{:S(2)}, u32[]{:S(2)}) async-start(bf16[16,256,256]{2,1,0:T(8,128)(2,1)} %shard_map.117), calls=%async_computation.2 | async-start | bytes 4194304 | tf_op jit(solution)/shard_map/all_to_all | solution.py:104
  410.4 10.0 copy-start.3
  420.4 48.1 %copy-start.4 = (s32[16]{0:T(128)S(1)}, s32[16]{0:T(128)}, u32[]{:S(2)}) copy-start(s32[16]{0:T(128)} %order.23) | copy-start | bytes 196
  469.5 93.8 %collective-permute-start.5 = (bf16[16,256,512]{2,1,0:T(8,128)(2,1)}, bf16[16,256,512]{2,1,0:T(8,128)(2,1)}, u32[]{:S(2)}, u32[]{:S(2)}) collective-permute-start(bf16[16,256,512]{2,1,0:T(8,128)(2,1)} %all-to-all-done.5.refs_0_), channel_id=1, source_target_pairs={{0,16},{16,0},{1,17},{17,1},{2,18},{18,2},{3,19},{19,3},{4,20},{20... | collective-permute-start | bytes 12582920 | tf_op jit(solution)/shard_map/ppermute | solution.py:105
  484.5 635.4 %collective-permute-start.4 = (bf16[16,256,512]{2,1,0:T(8,128)(2,1)}, bf16[16,256,512]{2,1,0:T(8,128)(2,1)}, u32[]{:S(2)}, u32[]{:S(2)}) collective-permute-start(bf16[16,256,512]{2,1,0:T(8,128)(2,1)} %all-to-all-done.4.refs_0_), channel_id=1, source_target_pairs={{0,16},{16,0},{1,17},{17,1},{2,18},{18,2},{3,19},{19,3},{4,20},{20... | collective-permute-start | bytes 12582920 | tf_op jit(solution)/shard_map/ppermute | solution.py:105
  485.1 892.8 %collective-permute-start.3 = (bf16[16,256,512]{2,1,0:T(8,128)(2,1)}, bf16[16,256,512]{2,1,0:T(8,128)(2,1)}, u32[]{:S(2)}, u32[]{:S(2)}) collective-permute-start(bf16[16,256,512]{2,1,0:T(8,128)(2,1)} %all-to-all-done.3.refs_0_), channel_id=1, source_target_pairs={{0,16},{16,0},{1,17},{17,1},{2,18},{18,2},{3,19},{19,3},{4,20},{20... | collective-permute-start | bytes 12582920 | tf_op jit(solution)/shard_map/ppermute | solution.py:105
  486.6 1085.7 %collective-permute-start.1 = (bf16[16,256,512]{2,1,0:T(8,128)(2,1)}, bf16[16,256,512]{2,1,0:T(8,128)(2,1)}, u32[]{:S(2)}, u32[]{:S(2)}) collective-permute-start(bf16[16,256,512]{2,1,0:T(8,128)(2,1)} %all-to-all-done.1.refs_0_), channel_id=1, source_target_pairs={{0,16},{16,0},{1,17},{17,1},{2,18},{18,2},{3,19},{19,3},{4,20},{20... | collective-permute-start | bytes 12582920 | tf_op jit(solution)/shard_map/ppermute | solution.py:105
  491.7 4.0 copy-start.5
  499.1 48.9 %copy-start.2 = (bf16[16,256,256]{2,1,0:T(8,128)(2,1)}, bf16[16,256,256]{2,1,0:T(8,128)(2,1)S(1)}, u32[]{:S(2)}) copy-start(bf16[16,256,256]{2,1,0:T(8,128)(2,1)S(1)} %all-to-all-done.2.refs_0_) | copy-start | bytes 6291460
  499.1 51.2 %all-to-all-start = ((bf16[16,256,128]{2,1,0:T(8,128)(2,1)}), bf16[16,256,128]{2,1,0:T(8,128)(2,1)}, u32[]{:S(2)}, u32[]{:S(2)}) async-start(bf16[16,256,128]{2,1,0:T(8,128)(2,1)} %shard_map.111), calls=%async_computation | async-start | bytes 2097152 | tf_op jit(solution)/shard_map/all_to_all | solution.py:104
  539.9 1195.0 %collective-permute-start.2 = (bf16[16,256,256]{2,1,0:T(8,128)(2,1)S(1)}, bf16[16,256,256]{2,1,0:T(8,128)(2,1)}, u32[]{:S(2)}, u32[]{:S(2)}) collective-permute-start(bf16[16,256,256]{2,1,0:T(8,128)(2,1)S(1)} %all-to-all-done.2.refs_0_), channel_id=1, source_target_pairs={{0,16},{16,0},{1,17},{17,1},{2,18},{18,2},{3,19},{19,3},{4,20},{20... | collective-permute-start | bytes 6291464 | tf_op jit(solution)/shard_map/ppermute | solution.py:105
  563.3 1237.1 %collective-permute-start = (bf16[16,256,128]{2,1,0:T(8,128)(2,1)}, bf16[16,256,128]{2,1,0:T(8,128)(2,1)}, u32[]{:S(2)}, u32[]{:S(2)}) collective-permute-start(bf16[16,256,128]{2,1,0:T(8,128)(2,1)} %all-to-all-done.refs_0_), channel_id=1, source_target_pairs={{0,16},{16,0},{1,17},{17,1},{2,18},{18,2},{3,19},{19,3},{4,20},{20... | collective-permute-start | bytes 3145736 | tf_op jit(solution)/shard_map/ppermute | solution.py:105
  1800.4 33.8 %copy-start.1 = (bf16[2,4,8192]{2,1,0:T(4,128)(2,1)S(1)}, bf16[2,4,8192]{2,1,0:T(4,128)(2,1)}, u32[]{:S(2)}) copy-start(bf16[2,4,8192]{2,1,0:T(4,128)(2,1)} %param.9) | copy-start | bytes 393220

commit v2 on v1

--- a/solution.py
+++ b/solution.py
@@ -33,41 +33,48 @@
     return settle_blocks(received, old_owner, devices)
 
 
-def turn_kernel(columns, held_ref, out_ref):
-    out_ref[0] = held_ref[...].T
-
-
-def turn_pieces(held, columns, first, count, half):
+def turn_kernel(columns, held_ref, *refs):
+    refs[-1][0] = held_ref[...].T
+
+
+def turn_pieces(held, columns, first, count, half, after):
     devices = columns.shape[0]
     return pl.pallas_call(
         turn_kernel,
         grid_spec=pltpu.PrefetchScalarGridSpec(
             num_scalar_prefetch=1,
             grid=(devices,),
-            in_specs=[pl.BlockSpec((count, half), lambda p, columns: (first // count, columns[p]))],
+            in_specs=[pl.BlockSpec((count, half), lambda p, columns: (first // count, columns[p]))]
+            + [pl.BlockSpec(memory_space=pl.ANY)] * len(after),
             out_specs=pl.BlockSpec((1, half, count), lambda p, columns: (p, 0, 0)),
         ),
         out_shape=jax.ShapeDtypeStruct((devices, half, count), held.dtype),
         cost_estimate=pl.CostEstimate(
             flops=0, bytes_accessed=4 * devices * half * count, transcendentals=0
         ),
-    )(columns, held)
+    )(columns, held, *after)
 
 
 def place_kernel(devices, half, height, first, count, order, which, *refs):
-    source, tile, sems = refs[0], refs[-2], refs[-1]
+    source, (tile, token, buffer, in_sems, out_sems) = refs[0], refs[-5:]
+    token[0] = 0
     row = pl.multiple_of(which[0] * half, half)
-    copies = []
+    loads, stores = [], []
     for c in range(devices):
-        copy = pltpu.make_async_copy(
-            source.at[order[c]],
+        load = pltpu.make_async_copy(source.at[order[c]], buffer.at[c], in_sems.at[c])
+        load.start()
+        loads.append(load)
+    for c in range(devices):
+        loads[c].wait()
+        store = pltpu.make_async_copy(
+            buffer.at[c],
             tile.at[pl.ds(row, half), pl.ds(c * height + first, count)],
-            sems.at[c],
+            out_sems.at[c],
         )
-        copy.start()
-        copies.append(copy)
-    for copy in copies:
-        copy.wait()
+        store.start()
+        stores.append(store)
+    for store in stores:
+        store.wait()
 
 
 def place_blocks(source, tile, order, which, height, first):
@@ -81,31 +88,42 @@
         aliases = {3: 0}
     return pl.pallas_call(
         functools.partial(place_kernel, devices, half, height, first, count),
-        out_shape=jax.ShapeDtypeStruct((2 * half, devices * height), source.dtype),
+        out_shape=(
+            jax.ShapeDtypeStruct((2 * half, devices * height), source.dtype),
+            jax.ShapeDtypeStruct((1,), jnp.int32),
+        ),
         in_specs=[smem, smem] + [anywhere] * (len(operands) - 2),
-        out_specs=anywhere,
-        scratch_shapes=[pltpu.SemaphoreType.DMA((devices,))],
+        out_specs=(anywhere, smem),
+        scratch_shapes=[
+            pltpu.VMEM((devices, half, count), source.dtype),
+            pltpu.SemaphoreType.DMA((devices,)),
+            pltpu.SemaphoreType.DMA((devices,)),
+        ],
         input_output_aliases=aliases,
+        compiler_params=pltpu.CompilerParams(vmem_limit_bytes=24 * 2**20),
         cost_estimate=pl.CostEstimate(
             flops=0, bytes_accessed=4 * devices * half * count, transcendentals=0
         ),
     )(*operands)
 
 
-def shared_tiles(qkv_held, gu_held, new_inverse, old_owner, devices):
+def shared_tiles(qkv_held, gu_held, new_inverse, old_owner, devices, work):
     mine = lax.axis_index("group")
     half = qkv_held.shape[1] // devices // 2
     columns = 2 * new_inverse.astype(jnp.int32) + mine
     chunks = [(1, 0, 512), (1, 512, 512), (1, 1024, 512), (0, 0, 512), (1, 1536, 256), (0, 512, 128)]
     held = (qkv_held, gu_held)
     tiles = [None, None]
-    for which, first, count in chunks:
-        sent = turn_pieces(held[which], columns, first, count, half)
+    tokens = []
+    for k, (which, first, count) in enumerate(chunks):
+        after = list(work[k]) + (tokens[k - 3] if k >= 3 else [])
+        sent = turn_pieces(held[which], columns, first, count, half, after)
         own = lax.all_to_all(sent, "gx", split_axis=0, concat_axis=0, tiled=True)
         other = lax.ppermute(own, "group", [(0, 1), (1, 0)])
         height = held[which].shape[0]
-        tiles[which] = place_blocks(own, tiles[which], old_owner, mine, height, first)
-        tiles[which] = place_blocks(other, tiles[which], old_owner, 1 - mine, height, first)
+        tile, token = place_blocks(own, tiles[which], old_owner, mine, height, first)
+        tiles[which], later = place_blocks(other, tile, old_owner, 1 - mine, height, first)
+        tokens.append([token, later])
     return tiles
 
 
@@ -121,11 +139,6 @@
     myself = lax.axis_index("gx")
     in_block = qkv_held.shape[1] // devices
     new_inverse = jnp.argsort(new_owner)
-    if groups == 2 and in_block == 512 and qkv_held.shape[0] == 640 and gu_held.shape[0] == 1792:
-        qkv_tiles, gu_tiles = shared_tiles(qkv_held, gu_held, new_inverse, old_owner, devices)
-    else:
-        qkv_tiles = plain_tiles(qkv_held, new_inverse, old_owner, devices)
-        gu_tiles = plain_tiles(gu_held, new_inverse, old_owner, devices)
     qkv_part = jnp.einsum("srd,cd->src", step_inputs, qkv_held, preferred_element_type=jnp.float32)
     projected = gathered_columns(qkv_part.astype(jnp.bfloat16), old_owner)
     gu_part = jnp.einsum("srd,cd->src", mlp_inputs, gu_held, preferred_element_type=jnp.float32)
@@ -190,6 +203,14 @@
         preferred_element_type=jnp.float32,
     )
     context = (numer / total[..., None]).astype(jnp.bfloat16).reshape(2, ROWS, H * HD)
+    if groups == 2 and in_block == 512 and qkv_held.shape[0] == 640 and gu_held.shape[0] == 1792:
+        work = ((), (), (projected,), (activation,), (pair_all, numer_parts), (context,))
+        qkv_tiles, gu_tiles = shared_tiles(
+            qkv_held, gu_held, new_inverse, old_owner, devices, work
+        )
+    else:
+        qkv_tiles = plain_tiles(qkv_held, new_inverse, old_owner, devices)
+        gu_tiles = plain_tiles(gu_held, new_inverse, old_owner, devices)
     return (context, activation, qkv_tiles, gu_tiles)
 
 

time: 1840 us -> 734 us (0.40)
  Pallas kernels: 1300 us -> 126 us
  blocking collectives: 113 us -> 290 us
  waiting for transfers between devices: 331 us -> 227 us
    pallas_call x12, Pallas kernels: 1230 us -> 55.7 us  [place_blocks(): pl.pallas_call(functools.partial(place_kernel, devices, half, height, fir...]
    all_to_all x6, waiting for transfers between devices: 318 us -> 102 us  [shared_tiles(): own = lax.all_to_all(sent, 'gx', split_axis=0, concat_axis=0, tiled=True)]
    all_gather x2, blocking collectives: 59.3 us -> 183 us  [gathered_columns(): blocks = lax.all_gather(part, 'gx')[old_owner]]
    ppermute x6, waiting for transfers between devices: 13.1 us -> 125 us  [shared_tiles(): other = lax.ppermute(own, 'group', [(0, 1), (1, 0)])]
    all_gather x1, blocking collectives: 18.1 us -> 89.3 us  [local(): numer_parts = lax.all_gather(local_numer.astype(jnp.bfloat16), 'gx')]
  transfers between devices with their start and end apart: 12 -> 12, of which waited for: 5 -> 5; matrix products, arithmetic and copies ran while one was open for 2% -> 6% of each run, Pallas kernels for 68% -> 15%
where the time goes in v2:
time: 734 us; the launch traced here: 731 us
  blocking collectives  290 us (40%)
  waiting for transfers between devices  227 us (31%)
  Pallas kernels  126 us (17%)
  starting transfers between devices  41.7 us (6%)
  matrix products  24.1 us (3%)
  local copies, waits for them, and re-layouts  17.1 us (2%)
    all_gather x2, blocking collectives, gathered_columns(): blocks = lax.all_gather(part, 'gx')[old_owner]  183 us
    ppermute x6, waiting for transfers between devices, shared_tiles(): other = lax.ppermute(own, 'group', [(0, 1), (1, 0)])  125 us
    all_to_all x6, waiting for transfers between devices, shared_tiles(): own = lax.all_to_all(sent, 'gx', split_axis=0, concat_axis=0, tiled=True)  102 us
    all_gather x1, blocking collectives, local(): numer_parts = lax.all_gather(local_numer.astype(jnp.bfloat16), 'gx')  89.3 us
    pallas_call x6, Pallas kernels, turn_pieces(): pl.pallas_call(turn_kernel, grid_spec=pltpu.PrefetchScalarGridSpec(num_sc...  70.3 us
    pallas_call x12, Pallas kernels, place_blocks(): pl.pallas_call(functools.partial(place_kernel, devices, half, height, fir...  55.7 us
    all_to_all x6, starting transfers between devices, shared_tiles(): own = lax.all_to_all(sent, 'gx', split_axis=0, concat_axis=0, tiled=True)  33.3 us
    all_gather x1, blocking collectives, local(): pair_all = lax.all_gather(jnp.stack([local_top, local_total]), 'gx')  18.2 us
  transfers between devices with their start and end apart: 12, of which 5 were waited for; matrix products, arithmetic and copies ran while one was open for 6% of the time, Pallas kernels for 15%

profile of v2, /device:TPU:8, one launch (start us, length us, event | category | flops | bytes accessed | tf_op | source)
XLA Modules:
  0.0 731.4 jit_solution(12251655042302398019)
XLA Ops:
  3.2 11.5 %shard_map.113 = bf16[16,256,512]{2,1,0:T(8,128)(2,1)} custom-call(s32[16]{0:T(128)} %multiply_add_fusion.columns, bf16[1792,8192]{1,0:T(8,128)(2,1)} %held_ref.11), custom_call_target="tpu_custom_call" | custom-call | bytes 8388608 | tf_op jit(solution)/shard_map/pallas_call | solution.py:42
  14.7 6.3 all-to-all-start.2
  20.9 11.5 %shard_map.112 = bf16[16,256,512]{2,1,0:T(8,128)(2,1)} custom-call(s32[16]{0:T(128)} %multiply_add_fusion.columns, bf16[1792,8192]{1,0:T(8,128)(2,1)} %held_ref.11), custom_call_target="tpu_custom_call" | custom-call | bytes 8388608 | tf_op jit(solution)/shard_map/pallas_call | solution.py:42
  32.5 79.3 %all-to-all-done.2.refs_0_ = bf16[16,256,512]{2,1,0:T(8,128)(2,1)} async-done(((bf16[16,256,512]{2,1,0:T(8,128)(2,1)}), bf16[16,256,512]{2,1,0:T(8,128)(2,1)}, u32[]{:S(2)}, u32[]{:S(2)}) %all-to-all-start.2) | async-done | bytes 4194336 | tf_op jit(solution)/shard_map/all_to_all | solution.py:121
  111.8 6.6 all-to-all-start.1
  118.3 6.9 fusion.12
  125.2 96.3 %all-gather = bf16[32,4,640]{2,1,0:T(4,128)(2,1)S(1)} all-gather(bf16[2,4,640]{2,1,0:T(4,128)(2,1)S(1)} %fusion.12), channel_id=2, replica_groups=mesh['group'=2,'gx'=16] {'gx'}, dimensions={0}, use_global_device_ids=true | all-gather | bytes 174080 | tf_op jit(solution)/shard_map/all_gather | solution.py:132
  222.9 11.5 %shard_map.111 = bf16[16,256,512]{2,1,0:T(8,128)(2,1)} custom-call(s32[16]{0:T(128)} %multiply_add_fusion.columns, bf16[1792,8192]{1,0:T(8,128)(2,1)} %held_ref.11, bf16[2,4,10240]{2,1,0:T(4,128)(2,1)} %bitcast.101), custom_call_target="tpu_custom_call" | custom-call | bytes 8388608 | tf_op jit(solution)/shard_map/pallas_call | solution.py:42
  234.5 4.5 all-to-all-start
  240.5 13.4 %fusion = f32[2,4,1792]{2,1,0:T(4,128)S(1)} fusion(bf16[2,4,8192]{2,1,0:T(4,128)(2,1)S(1)} %copy-done, bf16[1792,8192]{1,0:T(8,128)(2,1)} %held_ref.11), kind=kOutput, calls=%fused_computation.2 | convolution fusion | flops 234881024 | bytes 29548544 | tf_op jit(solution)/shard_map/srd,cd->src/dot_general | solution.py:144
  256.0 86.4 %all-gather.3 = bf16[32,4,896]{2,1,0:T(4,128)(2,1)S(1)} all-gather(bf16[2,4,896]{2,1,0:T(4,128)(2,1)S(1)} %fusion.31), channel_id=5, replica_groups=mesh['group'=2,'gx'=16] {'gx'}, dimensions={0}, use_global_device_ids=true | all-gather | bytes 243712 | tf_op jit(solution)/shard_map/all_gather | solution.py:132
  343.9 4.9 shard_map.114
  348.8 4.9 shard_map.115
  353.8 12.8 %shard_map.121 = bf16[16,256,512]{2,1,0:T(8,128)(2,1)} custom-call(s32[16]{0:T(128)} %multiply_add_fusion.columns, bf16[640,8192]{1,0:T(8,128)(2,1)} %held_ref.10, bf16[2,4,14336]{2,1,0:T(4,128)(2,1)} %bitcast.104, s32[1]{0:T(128)} %get-tuple-element.31.refs_1_, s32[1]{0:T(128)} %get-tuple-element.32.refs_2_), custom_call_target="tpu_custom_call" | custom-call | bytes 8388608 | tf_op jit(solution)/shard_map/pallas_call | solution.py:42
  366.6 4.8 all-to-all-start.4
  386.6 89.3 %all-gather.1 = bf16[32,8,8,128]{3,2,0,1:T(8,128)(2,1)S(1)} all-gather(bf16[2,8,8,128]{3,2,0,1:T(8,128)(2,1)S(1)} %fusion.11), channel_id=3, replica_groups=mesh['group'=2,'gx'=16] {'gx'}, dimensions={0}, use_global_device_ids=true | all-gather | bytes 557056 | tf_op jit(solution)/shard_map/all_gather | solution.py:178
  478.7 18.2 %all-gather.2 = f32[32,2,8,8]{3,2,1,0:T(8,128)} all-gather(f32[2,2,8,8]{3,2,1,0:T(8,128)S(1)} %pad_maximum_fusion), channel_id=4, replica_groups=mesh['group'=2,'gx'=16] {'gx'}, dimensions={0}, use_global_device_ids=true | all-gather | bytes 17408 | tf_op jit(solution)/shard_map/all_gather | solution.py:176
  496.9 4.9 shard_map.116
  501.8 4.9 shard_map.117
  506.8 11.8 %shard_map.126 = bf16[16,256,256]{2,1,0:T(8,128)(2,1)} custom-call(s32[16]{0:T(128)} %multiply_add_fusion.columns, bf16[1792,8192]{1,0:T(8,128)(2,1)} %held_ref.11, f32[4,4,2,2,8,8]{5,4,3,2,1,0:T(8,128)} %bitcast.98, bf16[4,4,2,8,8,128]{5,4,3,2,1,0:T(8,128)(2,1)} %bitcast.96, s32[1]{0:T(128)} %get-tuple-element.37.refs_2_, s32[1]{0:T(128)} %get-tuple-element.38.refs_3_), custom_call_target="tpu_custom_call" | custom-call | bytes 4194304 | tf_op jit(solution)/shard_map/pallas_call | solution.py:42
  518.6 6.9 all-to-all-start.5
  528.7 4.9 shard_map.118
  533.6 37.3 %collective-permute-done.2.refs_0_ = bf16[16,256,512]{2,1,0:T(8,128)(2,1)} collective-permute-done((bf16[16,256,512]{2,1,0:T(8,128)(2,1)}, bf16[16,256,512]{2,1,0:T(8,128)(2,1)}, u32[]{:S(2)}, u32[]{:S(2)}) %collective-permute-start.2) | collective-permute-done | bytes 4194336 | tf_op jit(solution)/shard_map/ppermute | solution.py:122
  570.9 4.9 shard_map.119
  575.8 11.2 %shard_map.120 = bf16[16,256,128]{2,1,0:T(8,128)(2,1)} custom-call(s32[16]{0:T(128)} %multiply_add_fusion.columns, bf16[640,8192]{1,0:T(8,128)(2,1)} %held_ref.10, bf16[2,4,8192]{2,1,0:T(4,128)(2,1)} %reshape.89.refs_0_, s32[1]{0:T(128)} %get-tuple-element.28.refs_1_, s32[1]{0:T(128)} %get-tuple-element.30.refs_2_), custom_call_target="tpu_custom_call" | custom-call | bytes 2097152 | tf_op jit(solution)/shard_map/pallas_call | solution.py:42
  587.0 4.3 all-to-all-start.3
  592.8 22.7 %all-to-all-done.3.refs_0_ = bf16[16,256,128]{2,1,0:T(8,128)(2,1)S(1)} async-done(((bf16[16,256,128]{2,1,0:T(8,128)(2,1)}), bf16[16,256,128]{2,1,0:T(8,128)(2,1)S(1)}, u32[]{:S(2)}, u32[]{:S(2)}) %all-to-all-start.3) | async-done | bytes 1048608 | tf_op jit(solution)/shard_map/all_to_all | solution.py:121
  617.0 5.4 shard_map.127
  622.5 83.3 %collective-permute-done.5.refs_0_ = bf16[16,256,256]{2,1,0:T(8,128)(2,1)} collective-permute-done((bf16[16,256,256]{2,1,0:T(8,128)(2,1)S(1)}, bf16[16,256,256]{2,1,0:T(8,128)(2,1)}, u32[]{:S(2)}, u32[]{:S(2)}) %collective-permute-start.5) | collective-permute-done | bytes 2097184 | tf_op jit(solution)/shard_map/ppermute | solution.py:122
  709.4 4.9 shard_map.122
  714.3 4.9 shard_map.123
  722.9 4.6 collective-permute-done.3.refs_0_
  (74 shorter events, 44.3 us)
Async XLA Ops:
  0.6 239.9 %copy-start = (bf16[2,4,8192]{2,1,0:T(4,128)(2,1)S(1)}, bf16[2,4,8192]{2,1,0:T(4,128)(2,1)}, u32[]{:S(2)}) copy-start(bf16[2,4,8192]{2,1,0:T(4,128)(2,1)} %param.9) | copy-start | bytes 393220
  14.7 97.1 %all-to-all-start.2 = ((bf16[16,256,512]{2,1,0:T(8,128)(2,1)}), bf16[16,256,512]{2,1,0:T(8,128)(2,1)}, u32[]{:S(2)}, u32[]{:S(2)}) async-start(bf16[16,256,512]{2,1,0:T(8,128)(2,1)} %shard_map.113), calls=%async_computation.2 | async-start | bytes 8388608 | tf_op jit(solution)/shard_map/all_to_all | solution.py:121
  32.5 85.9 %copy-start.6 = (bf16[2,4,8192]{2,1,0:T(4,128)(2,1)S(1)}, bf16[2,4,8192]{2,1,0:T(4,128)(2,1)}, u32[]{:S(2)}) copy-start(bf16[2,4,8192]{2,1,0:T(4,128)(2,1)} %param.8) | copy-start | bytes 393220
  111.8 122.7 %all-to-all-start.1 = ((bf16[16,256,512]{2,1,0:T(8,128)(2,1)}), bf16[16,256,512]{2,1,0:T(8,128)(2,1)}, u32[]{:S(2)}, u32[]{:S(2)}) async-start(bf16[16,256,512]{2,1,0:T(8,128)(2,1)} %shard_map.112), calls=%async_computation.1 | async-start | bytes 8388608 | tf_op jit(solution)/shard_map/all_to_all | solution.py:121
  118.3 103.2 %copy-start.2 = (s32[16]{0:T(128)S(1)}, s32[16]{0:T(128)}, u32[]{:S(2)}) copy-start(s32[16]{0:T(128)} %order.23) | copy-start | bytes 196
  234.5 132.1 %all-to-all-start = ((bf16[16,256,512]{2,1,0:T(8,128)(2,1)}), bf16[16,256,512]{2,1,0:T(8,128)(2,1)}, u32[]{:S(2)}, u32[]{:S(2)}) async-start(bf16[16,256,512]{2,1,0:T(8,128)(2,1)} %shard_map.111), calls=%async_computation | async-start | bytes 8388608 | tf_op jit(solution)/shard_map/all_to_all | solution.py:121
  238.9 109.9 %collective-permute-start.1 = (bf16[16,256,512]{2,1,0:T(8,128)(2,1)}, bf16[16,256,512]{2,1,0:T(8,128)(2,1)}, u32[]{:S(2)}, u32[]{:S(2)}) collective-permute-start(bf16[16,256,512]{2,1,0:T(8,128)(2,1)} %all-to-all-done.2.refs_0_), channel_id=1, source_target_pairs={{0,16},{16,0},{1,17},{17,1},{2,18},{18,2},{3,19},{19,3},{4,20},{20... | collective-permute-start | bytes 12582920 | tf_op jit(solution)/shard_map/ppermute | solution.py:122
  366.6 6.4 copy-start.5
  366.6 152.0 %all-to-all-start.4 = ((bf16[16,256,512]{2,1,0:T(8,128)(2,1)}), bf16[16,256,512]{2,1,0:T(8,128)(2,1)}, u32[]{:S(2)}, u32[]{:S(2)}) async-start(bf16[16,256,512]{2,1,0:T(8,128)(2,1)} %shard_map.121), calls=%async_computation.4 | async-start | bytes 8388608 | tf_op jit(solution)/shard_map/all_to_all | solution.py:121
  371.4 130.5 %collective-permute-start = (bf16[16,256,512]{2,1,0:T(8,128)(2,1)}, bf16[16,256,512]{2,1,0:T(8,128)(2,1)}, u32[]{:S(2)}, u32[]{:S(2)}) collective-permute-start(bf16[16,256,512]{2,1,0:T(8,128)(2,1)} %all-to-all-done.1.refs_0_), channel_id=1, source_target_pairs={{0,16},{16,0},{1,17},{17,1},{2,18},{18,2},{3,19},{19,3},{4,20},{20... | collective-permute-start | bytes 12582920 | tf_op jit(solution)/shard_map/ppermute | solution.py:122
  377.2 5.4 copy-start.7
  477.1 93.8 %collective-permute-start.2 = (bf16[16,256,512]{2,1,0:T(8,128)(2,1)}, bf16[16,256,512]{2,1,0:T(8,128)(2,1)}, u32[]{:S(2)}, u32[]{:S(2)}) collective-permute-start(bf16[16,256,512]{2,1,0:T(8,128)(2,1)} %all-to-all-done.refs_0_), channel_id=1, source_target_pairs={{0,16},{16,0},{1,17},{17,1},{2,18},{18,2},{3,19},{19,3},{4,20},{20... | collective-permute-start | bytes 12582920 | tf_op jit(solution)/shard_map/ppermute | solution.py:122
  518.6 7.0 copy-start.4
  518.6 8.7 %copy-start.3 = (bf16[32,8,8,128]{3,2,1,0:T(8,128)(2,1)S(1)}, bf16[32,8,8,128]{3,2,1,0:T(8,128)(2,1)}, u32[]{:S(2)}) copy-start(bf16[32,8,8,128]{3,2,1,0:T(8,128)(2,1)} %copy.73) | copy-start | bytes 1572868
  518.6 68.4 %all-to-all-start.5 = ((bf16[16,256,256]{2,1,0:T(8,128)(2,1)}), bf16[16,256,256]{2,1,0:T(8,128)(2,1)S(1)}, u32[]{:S(2)}, u32[]{:S(2)}) async-start(bf16[16,256,256]{2,1,0:T(8,128)(2,1)} %shard_map.126), calls=%async_computation.5 | async-start | bytes 4194304 | tf_op jit(solution)/shard_map/all_to_all | solution.py:121
  526.3 188.0 %collective-permute-start.4 = (bf16[16,256,512]{2,1,0:T(8,128)(2,1)}, bf16[16,256,512]{2,1,0:T(8,128)(2,1)}, u32[]{:S(2)}, u32[]{:S(2)}) collective-permute-start(bf16[16,256,512]{2,1,0:T(8,128)(2,1)} %all-to-all-done.4.refs_0_), channel_id=1, source_target_pairs={{0,16},{16,0},{1,17},{17,1},{2,18},{18,2},{3,19},{19,3},{4,20},{20... | collective-permute-start | bytes 12582920 | tf_op jit(solution)/shard_map/ppermute | solution.py:122
  587.0 28.5 %all-to-all-start.3 = ((bf16[16,256,128]{2,1,0:T(8,128)(2,1)}), bf16[16,256,128]{2,1,0:T(8,128)(2,1)S(1)}, u32[]{:S(2)}, u32[]{:S(2)}) async-start(bf16[16,256,128]{2,1,0:T(8,128)(2,1)} %shard_map.120), calls=%async_computation.3 | async-start | bytes 2097152 | tf_op jit(solution)/shard_map/all_to_all | solution.py:121
  591.3 114.4 %collective-permute-start.5 = (bf16[16,256,256]{2,1,0:T(8,128)(2,1)S(1)}, bf16[16,256,256]{2,1,0:T(8,128)(2,1)}, u32[]{:S(2)}, u32[]{:S(2)}) collective-permute-start(bf16[16,256,256]{2,1,0:T(8,128)(2,1)S(1)} %all-to-all-done.5.refs_0_), channel_id=1, source_target_pairs={{0,16},{16,0},{1,17},{17,1},{2,18},{18,2},{3,19},{19,3},{4,20},{20... | collective-permute-start | bytes 6291464 | tf_op jit(solution)/shard_map/ppermute | solution.py:122
  615.5 112.0 %collective-permute-start.3 = (bf16[16,256,128]{2,1,0:T(8,128)(2,1)S(1)}, bf16[16,256,128]{2,1,0:T(8,128)(2,1)S(1)}, u32[]{:S(2)}, u32[]{:S(2)}) collective-permute-start(bf16[16,256,128]{2,1,0:T(8,128)(2,1)S(1)} %all-to-all-done.3.refs_0_), channel_id=1, source_target_pairs={{0,16},{16,0},{1,17},{17,1},{2,18},{18,2},{3,19},{19,3},{4,20},{20... | collective-permute-start | bytes 3145736 | tf_op jit(solution)/shard_map/ppermute | solution.py:122
  727.5 3.7 copy-start.1

commit v3 on v2

--- a/solution.py
+++ b/solution.py
@@ -77,7 +77,7 @@
         store.wait()
 
 
-def place_blocks(source, tile, order, which, height, first):
+def place_blocks(source, tile, order, which, height, first, block):
     devices, half, count = source.shape
     smem = pl.BlockSpec(memory_space=pltpu.SMEM)
     anywhere = pl.BlockSpec(memory_space=pl.ANY)
@@ -89,7 +89,7 @@
     return pl.pallas_call(
         functools.partial(place_kernel, devices, half, height, first, count),
         out_shape=(
-            jax.ShapeDtypeStruct((2 * half, devices * height), source.dtype),
+            jax.ShapeDtypeStruct((block, devices * height), source.dtype),
             jax.ShapeDtypeStruct((1,), jnp.int32),
         ),
         in_specs=[smem, smem] + [anywhere] * (len(operands) - 2),
@@ -107,30 +107,72 @@
     )(*operands)
 
 
-def shared_tiles(qkv_held, gu_held, new_inverse, old_owner, devices, work):
-    mine = lax.axis_index("group")
-    half = qkv_held.shape[1] // devices // 2
-    columns = 2 * new_inverse.astype(jnp.int32) + mine
-    chunks = [(1, 0, 512), (1, 512, 512), (1, 1024, 512), (0, 0, 512), (1, 1536, 256), (0, 512, 128)]
-    held = (qkv_held, gu_held)
-    tiles = [None, None]
-    tokens = []
-    for k, (which, first, count) in enumerate(chunks):
-        after = list(work[k]) + (tokens[k - 3] if k >= 3 else [])
-        sent = turn_pieces(held[which], columns, first, count, half, after)
+def hold_kernel(value_ref, *refs):
+    refs[-1][...] = value_ref[...]
+
+
+def hold(value, after):
+    vmem = pl.BlockSpec(memory_space=pltpu.VMEM)
+    return pl.pallas_call(
+        hold_kernel,
+        out_shape=jax.ShapeDtypeStruct(value.shape, value.dtype),
+        in_specs=[vmem] + [pl.BlockSpec(memory_space=pl.ANY)] * len(after),
+        out_specs=vmem,
+    )(value, *after)
+
+
+def three_parts(value):
+    high = lax.reduce_precision(value, 8, 7)
+    middle = lax.reduce_precision(value - high, 8, 7)
+    low = value - high - middle
+    return jnp.stack([high, middle, low]).astype(jnp.bfloat16)
+
+
+chunks = (
+    (1, 0, 512, True),
+    (1, 512, 512, True),
+    (1, 1024, 512, True),
+    (0, 0, 512, True),
+    (1, 1536, 256, True),
+    (0, 512, 128, False),
+)
+
+
+class Retiling:
+    def __init__(self, held, new_inverse, old_owner, devices):
+        self.held, self.old_owner = held, old_owner
+        self.inverse = new_inverse.astype(jnp.int32)
+        self.mine = lax.axis_index("group")
+        self.block = held[0].shape[1] // devices
+        self.tiles = [None, None]
+        self.sent, self.own, self.tokens = [], [], []
+
+    def send(self, after):
+        which, first, count, halves = chunks[len(self.sent)]
+        held, mine = self.held[which], self.mine
+        half = self.block // 2 if halves else self.block
+        columns = 2 * self.inverse + mine if halves else self.inverse
+        sent = turn_pieces(held, columns, first, count, half, after)
         own = lax.all_to_all(sent, "gx", split_axis=0, concat_axis=0, tiled=True)
-        other = lax.ppermute(own, "group", [(0, 1), (1, 0)])
-        height = held[which].shape[0]
-        tile, token = place_blocks(own, tiles[which], old_owner, mine, height, first)
-        tiles[which], later = place_blocks(other, tile, old_owner, 1 - mine, height, first)
-        tokens.append([token, later])
-    return tiles
-
-
-def gathered_columns(part, old_owner):
-    steps, rows, width = part.shape
-    blocks = lax.all_gather(part, "gx")[old_owner]
-    return jnp.moveaxis(blocks, 0, 2).reshape(steps, rows, -1)
+        place = functools.partial(
+            place_blocks, order=self.old_owner, height=held.shape[0], first=first, block=self.block
+        )
+        where = mine if halves else jnp.zeros((), jnp.int32)
+        tile, token = place(own, self.tiles[which], which=where)
+        tokens = [token]
+        if halves:
+            other = lax.ppermute(own, "group", [(0, 1), (1, 0)])
+            tile, token = place(other, tile, which=1 - mine)
+            tokens.append(token)
+        self.tiles[which] = tile
+        self.sent.append(sent)
+        self.own.append(own)
+        self.tokens.append(tokens)
+
+
+def side_by_side(blocks, old_owner):
+    _, steps, rows, _ = blocks.shape
+    return jnp.moveaxis(blocks[old_owner], 0, 2).reshape(steps, rows, -1)
 
 
 def local(step_inputs, mlp_inputs, qkv_held, gu_held, old_owner, new_owner, kv_cache, lengths):
@@ -139,11 +181,22 @@
     myself = lax.axis_index("gx")
     in_block = qkv_held.shape[1] // devices
     new_inverse = jnp.argsort(new_owner)
+    shared = (
+        groups == 2 and in_block == 512 and qkv_held.shape[0] == 640 and gu_held.shape[0] == 1792
+    )
     qkv_part = jnp.einsum("srd,cd->src", step_inputs, qkv_held, preferred_element_type=jnp.float32)
-    projected = gathered_columns(qkv_part.astype(jnp.bfloat16), old_owner)
     gu_part = jnp.einsum("srd,cd->src", mlp_inputs, gu_held, preferred_element_type=jnp.float32)
     activated = (jax.nn.silu(gu_part[..., 0::2]) * gu_part[..., 1::2]).astype(jnp.bfloat16)
-    activation = gathered_columns(activated, old_owner)
+    parts = jnp.concatenate([qkv_part.astype(jnp.bfloat16), activated], axis=2)
+    if shared:
+        retiling = Retiling((qkv_held, gu_held), new_inverse, old_owner, devices)
+        retiling.send(())
+        retiling.send(())
+        retiling.send((retiling.own[0],))
+        parts = hold(parts, (retiling.sent[2],))
+    part_blocks = lax.all_gather(parts, "gx")
+    projected = side_by_side(part_blocks[..., : qkv_held.shape[0]], old_owner)
+    activation = side_by_side(part_blocks[..., qkv_held.shape[0] :], old_owner)
     score_scale = 1.0 / HD**0.5
     group_size = H // KVH
     local_tokens = kv_cache.shape[0]
@@ -173,11 +226,25 @@
         preferred_element_type=jnp.float32,
     )
     shards = CTX // local_tokens
-    pair_all = lax.all_gather(jnp.stack([local_top, local_total]), "gx")
-    pair_all = pair_all.reshape(ROWS, shards, 2, 2, KVH, group_size)
-    numer_parts = lax.all_gather(local_numer.astype(jnp.bfloat16), "gx")
-    numer_parts = numer_parts.reshape(ROWS, shards, 2, KVH, group_size, HD)
-    tops, totals = pair_all[:, :, 0], pair_all[:, :, 1]
+    count = local_numer.size // HD
+    packed = jnp.concatenate(
+        [
+            local_numer.astype(jnp.bfloat16).reshape(count, HD),
+            three_parts(local_top).reshape(-1, HD),
+            three_parts(local_total).reshape(-1, HD),
+        ]
+    )
+    used = packed.shape[0]
+    packed = jnp.pad(packed, ((0, -used % 16), (0, 0)))
+    if shared:
+        retiling.send((retiling.own[1],))
+        packed = hold(packed, (retiling.sent[3],))
+    everyone = lax.all_gather(packed, "gx")
+    numer_parts = everyone[:, :count].reshape(ROWS, shards, 2, KVH, group_size, HD)
+    pairs = everyone[:, count:used].astype(jnp.float32).reshape(devices, 2, 3, -1)
+    pairs = (pairs[:, :, 0] + pairs[:, :, 1]) + pairs[:, :, 2]
+    pairs = pairs.reshape(ROWS, shards, 2, 2, KVH, group_size)
+    tops, totals = pairs[:, :, 0], pairs[:, :, 1]
     top_all = jnp.max(tops, axis=1)
     factors = jnp.exp(tops - top_all[:, None])
     total_all = jnp.moveaxis(jnp.sum(totals * factors, axis=1), 0, 1)
@@ -203,11 +270,10 @@
         preferred_element_type=jnp.float32,
     )
     context = (numer / total[..., None]).astype(jnp.bfloat16).reshape(2, ROWS, H * HD)
-    if groups == 2 and in_block == 512 and qkv_held.shape[0] == 640 and gu_held.shape[0] == 1792:
-        work = ((), (), (projected,), (activation,), (pair_all, numer_parts), (context,))
-        qkv_tiles, gu_tiles = shared_tiles(
-            qkv_held, gu_held, new_inverse, old_owner, devices, work
-        )
+    if shared:
+        retiling.send((retiling.own[2], *retiling.tokens[0]))
+        retiling.send((retiling.own[3], context, activation, *retiling.tokens[1]))
+        qkv_tiles, gu_tiles = retiling.tiles
     else:
         qkv_tiles = plain_tiles(qkv_held, new_inverse, old_owner, devices)
         gu_tiles = plain_tiles(gu_held, new_inverse, old_owner, devices)

time: 734 us -> 757 us (1.031)
  waiting for transfers between devices: 227 us -> 460 us
  blocking collectives: 290 us -> 65.5 us
    all_gather x4 -> x2, blocking collectives: 290 us -> 65.5 us  [the longest x1 46.9 us: local(): part_blocks = lax.all_gather(parts, 'gx')]
    all_to_all x6, waiting for transfers between devices: 102 us -> 238 us  [send(): own = lax.all_to_all(sent, 'gx', split_axis=0, concat_axis=0, tiled=True)]
    ppermute x6 -> x5, waiting for transfers between devices: 125 us -> 222 us  [send(): other = lax.ppermute(own, 'group', [(0, 1), (1, 0)])]
    pallas_call x12 -> x11, Pallas kernels: 55.7 us -> 52 us  [place_blocks(): pl.pallas_call(functools.partial(place_kernel, devices, half, height, fir...]
  transfers between devices with their start and end apart: 12 -> 11, of which waited for: 5 -> 7; matrix products, arithmetic and copies ran while one was open for 6% -> 7% of each run, Pallas kernels for 15% -> 15%
where the time goes in v3:
time: 757 us; the launch traced here: 750 us
  waiting for transfers between devices  460 us (61%)
  Pallas kernels  125 us (17%)
  blocking collectives  65.5 us (9%)
  starting transfers between devices  45.1 us (6%)
  matrix products  26.5 us (4%)
  local copies, waits for them, and re-layouts  22.5 us (3%)
    all_to_all x6, waiting for transfers between devices, send(): own = lax.all_to_all(sent, 'gx', split_axis=0, concat_axis=0, tiled=True)  238 us
    ppermute x5, waiting for transfers between devices, send(): other = lax.ppermute(own, 'group', [(0, 1), (1, 0)])  222 us
    pallas_call x6, Pallas kernels, turn_pieces(): pl.pallas_call(turn_kernel, grid_spec=pltpu.PrefetchScalarGridSpec(num_sc...  69.8 us
    pallas_call x11, Pallas kernels, place_blocks(): pl.pallas_call(functools.partial(place_kernel, devices, half, height, fir...  52 us
    all_gather x1, blocking collectives, local(): part_blocks = lax.all_gather(parts, 'gx')  46.9 us
    all_to_all x6, starting transfers between devices, send(): own = lax.all_to_all(sent, 'gx', split_axis=0, concat_axis=0, tiled=True)  39.4 us
    all_gather x1, blocking collectives, local(): everyone = lax.all_gather(packed, 'gx')  18.6 us
  transfers between devices with their start and end apart: 11, of which 7 were waited for; matrix products, arithmetic and copies ran while one was open for 7% of the time, Pallas kernels for 15%

profile of v3, /device:TPU:8, one launch (start us, length us, event | category | flops | bytes accessed | tf_op | source)
XLA Modules:
  0.0 750.2 jit_solution(12658953721366851965)
XLA Ops:
  3.1 11.5 %shard_map.111 = bf16[16,256,512]{2,1,0:T(8,128)(2,1)} custom-call(s32[16]{0:T(128)} %multiply_add_fusion.columns, bf16[1792,8192]{1,0:T(8,128)(2,1)} %held_ref.11), custom_call_target="tpu_custom_call" | custom-call | bytes 8388608 | tf_op jit(solution)/shard_map/pallas_call | solution.py:42
  14.6 6.3 all-to-all-start
  20.9 11.5 %shard_map.114 = bf16[16,256,512]{2,1,0:T(8,128)(2,1)} custom-call(s32[16]{0:T(128)} %multiply_add_fusion.columns, bf16[1792,8192]{1,0:T(8,128)(2,1)} %held_ref.11), custom_call_target="tpu_custom_call" | custom-call | bytes 8388608 | tf_op jit(solution)/shard_map/pallas_call | solution.py:42
  32.4 79.3 %all-to-all-done.refs_0_ = bf16[16,256,512]{2,1,0:T(8,128)(2,1)} async-done(((bf16[16,256,512]{2,1,0:T(8,128)(2,1)}), bf16[16,256,512]{2,1,0:T(8,128)(2,1)}, u32[]{:S(2)}, u32[]{:S(2)}) %all-to-all-start) | async-done | bytes 4194336 | tf_op jit(solution)/shard_map/all_to_all | solution.py:156
  111.7 6.6 all-to-all-start.1
  118.3 11.5 %shard_map.112.refs_0_ = bf16[16,256,512]{2,1,0:T(8,128)(2,1)} custom-call(s32[16]{0:T(128)} %multiply_add_fusion.columns, bf16[1792,8192]{1,0:T(8,128)(2,1)} %held_ref.11, bf16[16,256,512]{2,1,0:T(8,128)(2,1)} %all-to-all-done.refs_0_), custom_call_target="tpu_custom_call" | custom-call | bytes 8388608 | tf_op jit(solution)/shard_map/pallas_call | solution.py:42
  129.8 79.3 %all-to-all-done.1.refs_0_ = bf16[16,256,512]{2,1,0:T(8,128)(2,1)} async-done(((bf16[16,256,512]{2,1,0:T(8,128)(2,1)}), bf16[16,256,512]{2,1,0:T(8,128)(2,1)}, u32[]{:S(2)}, u32[]{:S(2)}) %all-to-all-start.1) | async-done | bytes 4194336 | tf_op jit(solution)/shard_map/all_to_all | solution.py:156
  209.1 6.6 all-to-all-start.4
  215.6 11.5 %shard_map.115.refs_0_ = bf16[16,256,512]{2,1,0:T(8,128)(2,1)} custom-call(s32[16]{0:T(128)} %multiply_add_fusion.columns, bf16[640,8192]{1,0:T(8,128)(2,1)} %held_ref.10, bf16[16,256,512]{2,1,0:T(8,128)(2,1)} %all-to-all-done.1.refs_0_), custom_call_target="tpu_custom_call" | custom-call | bytes 8388608 | tf_op jit(solution)/shard_map/pallas_call | solution.py:42
  227.2 79.3 %all-to-all-done.4.refs_0_ = bf16[16,256,512]{2,1,0:T(8,128)(2,1)} async-done(((bf16[16,256,512]{2,1,0:T(8,128)(2,1)}), bf16[16,256,512]{2,1,0:T(8,128)(2,1)}, u32[]{:S(2)}, u32[]{:S(2)}) %all-to-all-start.4) | async-done | bytes 4194336 | tf_op jit(solution)/shard_map/all_to_all | solution.py:156
  306.5 6.6 all-to-all-start.2
  319.8 6.9 fusion.12
  326.7 13.4 %fusion = f32[2,4,1792]{2,1,0:T(4,128)S(1)} fusion(bf16[2,4,8192]{2,1,0:T(4,128)(2,1)S(1)} %copy-done, bf16[1792,8192]{1,0:T(8,128)(2,1)} %held_ref.11), kind=kOutput, calls=%fused_computation.2 | convolution fusion | flops 234881024 | bytes 29548544 | tf_op jit(solution)/shard_map/srd,cd->src/dot_general | solution.py:188
  341.3 4.9 shard_map.117
  346.2 60.5 %collective-permute-done.refs_0_ = bf16[16,256,512]{2,1,0:T(8,128)(2,1)} collective-permute-done((bf16[16,256,512]{2,1,0:T(8,128)(2,1)}, bf16[16,256,512]{2,1,0:T(8,128)(2,1)}, u32[]{:S(2)}, u32[]{:S(2)}) %collective-permute-start) | collective-permute-done | bytes 4194336 | tf_op jit(solution)/shard_map/ppermute | solution.py:164
  406.7 4.9 shard_map.118
  411.7 11.9 %shard_map.125 = bf16[16,256,256]{2,1,0:T(8,128)(2,1)} custom-call(s32[16]{0:T(128)} %multiply_add_fusion.columns, bf16[1792,8192]{1,0:T(8,128)(2,1)} %held_ref.11, bf16[16,256,512]{2,1,0:T(8,128)(2,1)} %all-to-all-done.4.refs_0_, s32[1]{0:T(128)} %get-tuple-element.29.refs_1_, s32[1]{0:T(128)} %get-tuple-element.30.refs_2_), custom_call_target="tpu_custom_call" | custom-call | bytes 4194304 | tf_op jit(solution)/shard_map/pallas_call | solution.py:42
  423.6 6.0 all-to-all-start.5
  441.6 46.9 %all-gather = bf16[32,4,1536]{2,1,0:T(4,128)(2,1)S(1)} all-gather(bf16[2,4,1536]{2,1,0:T(4,128)(2,1)} %shard_map.113), channel_id=2, replica_groups=mesh['group'=2,'gx'=16] {'gx'}, dimensions={0}, use_global_device_ids=true | all-gather | bytes 417792 | tf_op jit(solution)/shard_map/all_gather | solution.py:197
  497.2 18.6 %all-gather.1 = bf16[2304,128]{1,0:T(8,128)(2,1)S(1)} all-gather(bf16[144,128]{1,0:T(8,128)(2,1)} %shard_map.116), channel_id=3, replica_groups=mesh['group'=2,'gx'=16] {'gx'}, dimensions={0}, use_global_device_ids=true | all-gather | bytes 626688 | tf_op jit(solution)/shard_map/all_gather | solution.py:242
  525.1 4.9 shard_map.119
  530.1 4.9 shard_map.120
  535.0 11.8 %shard_map.121 = bf16[16,512,128]{2,1,0:T(8,128)(2,1)} custom-call(s32[16]{0:T(128)} %copy-done.6, bf16[640,8192]{1,0:T(8,128)(2,1)} %held_ref.10, bf16[16,256,512]{2,1,0:T(8,128)(2,1)} %all-to-all-done.2.refs_0_, bf16[2,4,8192]{2,1,0:T(4,128)(2,1)} %reshape.178.refs_1_, bf16[2,4,14336]{2,1,0:T(4,128)(2,1)} %bitcast.101, s32[1]{0:T(128)} %get-tuple-element.23.refs_3_, ...), custom_call_target="tpu_custom_call" | custom-call | bytes 4194304 | tf_op jit(solution)/shard_map/pallas_call | solution.py:42
  546.8 7.4 all-to-all-start.3
  555.8 4.9 shard_map.122
  560.7 4.9 shard_map.126
  565.6 46.5 %collective-permute-done.4.refs_0_ = bf16[16,256,512]{2,1,0:T(8,128)(2,1)} collective-permute-done((bf16[16,256,512]{2,1,0:T(8,128)(2,1)}, bf16[16,256,512]{2,1,0:T(8,128)(2,1)}, u32[]{:S(2)}, u32[]{:S(2)}) %collective-permute-start.4) | collective-permute-done | bytes 4194336 | tf_op jit(solution)/shard_map/ppermute | solution.py:164
  612.2 4.9 shard_map.127
  617.1 5.4 shard_map.128
  622.5 79.6 %collective-permute-done.2.refs_0_ = bf16[16,256,512]{2,1,0:T(8,128)(2,1)} collective-permute-done((bf16[16,256,512]{2,1,0:T(8,128)(2,1)}, bf16[16,256,512]{2,1,0:T(8,128)(2,1)}, u32[]{:S(2)}, u32[]{:S(2)}) %collective-permute-start.2) | collective-permute-done | bytes 4194336 | tf_op jit(solution)/shard_map/ppermute | solution.py:164
  702.0 4.9 shard_map.123
  710.6 35.8 %collective-permute-done.3.refs_0_ = bf16[16,256,256]{2,1,0:T(8,128)(2,1)} collective-permute-done((bf16[16,256,256]{2,1,0:T(8,128)(2,1)S(1)}, bf16[16,256,256]{2,1,0:T(8,128)(2,1)}, u32[]{:S(2)}, u32[]{:S(2)}) %collective-permute-start.3) | collective-permute-done | bytes 2097184 | tf_op jit(solution)/shard_map/ppermute | solution.py:164
  (85 shorter events, 49.1 us)
Async XLA Ops:
  0.6 326.1 %copy-start = (bf16[2,4,8192]{2,1,0:T(4,128)(2,1)S(1)}, bf16[2,4,8192]{2,1,0:T(4,128)(2,1)}, u32[]{:S(2)}) copy-start(bf16[2,4,8192]{2,1,0:T(4,128)(2,1)} %param.9) | copy-start | bytes 393220
  2.6 12.0 %copy-start.6 = (s32[16]{0:T(128)}, s32[16]{0:T(128)S(1)}, u32[]{:S(2)}) copy-start(s32[16]{0:T(128)S(1)} %get-tuple-element.20.columns) | copy-start | bytes 196
  14.6 97.1 %all-to-all-start = ((bf16[16,256,512]{2,1,0:T(8,128)(2,1)}), bf16[16,256,512]{2,1,0:T(8,128)(2,1)}, u32[]{:S(2)}, u32[]{:S(2)}) async-start(bf16[16,256,512]{2,1,0:T(8,128)(2,1)} %shard_map.111), calls=%async_computation | async-start | bytes 8388608 | tf_op jit(solution)/shard_map/all_to_all | solution.py:156
  111.7 97.4 %all-to-all-start.1 = ((bf16[16,256,512]{2,1,0:T(8,128)(2,1)}), bf16[16,256,512]{2,1,0:T(8,128)(2,1)}, u32[]{:S(2)}, u32[]{:S(2)}) async-start(bf16[16,256,512]{2,1,0:T(8,128)(2,1)} %shard_map.114), calls=%async_computation.1 | async-start | bytes 8388608 | tf_op jit(solution)/shard_map/all_to_all | solution.py:156
  209.1 97.4 %all-to-all-start.4 = ((bf16[16,256,512]{2,1,0:T(8,128)(2,1)}), bf16[16,256,512]{2,1,0:T(8,128)(2,1)}, u32[]{:S(2)}, u32[]{:S(2)}) async-start(bf16[16,256,512]{2,1,0:T(8,128)(2,1)} %shard_map.112.refs_0_), calls=%async_computation.4 | async-start | bytes 8388608 | tf_op jit(solution)/shard_map/all_to_all | solution.py:156
  227.2 87.4 %copy-start.7 = (s32[4]{0:T(128)S(1)}, s32[4]{0:T(128)}, u32[]{:S(2)}) copy-start(s32[4]{0:T(128)} %param.15) | copy-start | bytes 52
  227.2 88.0 %copy-start.2 = (s32[16]{0:T(128)S(1)}, s32[16]{0:T(128)}, u32[]{:S(2)}) copy-start(s32[16]{0:T(128)} %order.21) | copy-start | bytes 196
  306.5 117.1 %all-to-all-start.2 = ((bf16[16,256,512]{2,1,0:T(8,128)(2,1)}), bf16[16,256,512]{2,1,0:T(8,128)(2,1)}, u32[]{:S(2)}, u32[]{:S(2)}) async-start(bf16[16,256,512]{2,1,0:T(8,128)(2,1)} %shard_map.115.refs_0_), calls=%async_computation.2 | async-start | bytes 8388608 | tf_op jit(solution)/shard_map/all_to_all | solution.py:156
  313.0 93.7 %collective-permute-start = (bf16[16,256,512]{2,1,0:T(8,128)(2,1)}, bf16[16,256,512]{2,1,0:T(8,128)(2,1)}, u32[]{:S(2)}, u32[]{:S(2)}) collective-permute-start(bf16[16,256,512]{2,1,0:T(8,128)(2,1)} %all-to-all-done.refs_0_), channel_id=1, source_target_pairs={{0,16},{16,0},{1,17},{17,1},{2,18},{18,2},{3,19},{19,3},{4,20},{20... | collective-permute-start | bytes 12582920 | tf_op jit(solution)/shard_map/ppermute | solution.py:164
  315.1 4.7 copy-start.4
  340.1 190.0 %collective-permute-start.1 = (bf16[16,256,512]{2,1,0:T(8,128)(2,1)}, bf16[16,256,512]{2,1,0:T(8,128)(2,1)}, u32[]{:S(2)}, u32[]{:S(2)}) collective-permute-start(bf16[16,256,512]{2,1,0:T(8,128)(2,1)} %all-to-all-done.1.refs_0_), channel_id=1, source_target_pairs={{0,16},{16,0},{1,17},{17,1},{2,18},{18,2},{3,19},{19,3},{4,20},{20... | collective-permute-start | bytes 12582920 | tf_op jit(solution)/shard_map/ppermute | solution.py:164
  423.6 123.2 %all-to-all-start.5 = ((bf16[16,256,256]{2,1,0:T(8,128)(2,1)}), bf16[16,256,256]{2,1,0:T(8,128)(2,1)S(1)}, u32[]{:S(2)}, u32[]{:S(2)}) async-start(bf16[16,256,256]{2,1,0:T(8,128)(2,1)} %shard_map.125), calls=%async_computation.5 | async-start | bytes 4194304 | tf_op jit(solution)/shard_map/all_to_all | solution.py:156
  489.4 0.7 copy-start.3
  518.1 2.4 copy-start.5
  518.4 93.8 %collective-permute-start.4 = (bf16[16,256,512]{2,1,0:T(8,128)(2,1)}, bf16[16,256,512]{2,1,0:T(8,128)(2,1)}, u32[]{:S(2)}, u32[]{:S(2)}) collective-permute-start(bf16[16,256,512]{2,1,0:T(8,128)(2,1)} %all-to-all-done.4.refs_0_), channel_id=1, source_target_pairs={{0,16},{16,0},{1,17},{17,1},{2,18},{18,2},{3,19},{19,3},{4,20},{20... | collective-permute-start | bytes 12582920 | tf_op jit(solution)/shard_map/ppermute | solution.py:164
  520.0 182.1 %collective-permute-start.2 = (bf16[16,256,512]{2,1,0:T(8,128)(2,1)}, bf16[16,256,512]{2,1,0:T(8,128)(2,1)}, u32[]{:S(2)}, u32[]{:S(2)}) collective-permute-start(bf16[16,256,512]{2,1,0:T(8,128)(2,1)} %all-to-all-done.2.refs_0_), channel_id=1, source_target_pairs={{0,16},{16,0},{1,17},{17,1},{2,18},{18,2},{3,19},{19,3},{4,20},{20... | collective-permute-start | bytes 12582920 | tf_op jit(solution)/shard_map/ppermute | solution.py:164
  546.8 160.1 %all-to-all-start.3 = ((bf16[16,512,128]{2,1,0:T(8,128)(2,1)}), bf16[16,512,128]{2,1,0:T(8,128)(2,1)}, u32[]{:S(2)}, u32[]{:S(2)}) async-start(bf16[16,512,128]{2,1,0:T(8,128)(2,1)} %shard_map.121), calls=%async_computation.3 | async-start | bytes 4194304 | tf_op jit(solution)/shard_map/all_to_all | solution.py:156
  554.3 192.1 %collective-permute-start.3 = (bf16[16,256,256]{2,1,0:T(8,128)(2,1)S(1)}, bf16[16,256,256]{2,1,0:T(8,128)(2,1)}, u32[]{:S(2)}, u32[]{:S(2)}) collective-permute-start(bf16[16,256,256]{2,1,0:T(8,128)(2,1)S(1)} %all-to-all-done.5.refs_0_), channel_id=1, source_target_pairs={{0,16},{16,0},{1,17},{17,1},{2,18},{18,2},{3,19},{19,3},{4,20},{20... | collective-permute-start | bytes 6291464 | tf_op jit(solution)/shard_map/ppermute | solution.py:164
  746.4 3.6 copy-start.1
